TPU v7x, 32 devices: a whole 2x2x4 slice. The times are simulated.
32 devices in a mesh: depth: 4 (over z), rows: 8 (over y, x, core).
Axes of the slice: x: 2, y: 2, z: 4, core: 2. Of those that a mesh axis runs over, the one named last changes fastest.
Arguments:
- in_flight: float32 [4, 2, 1024, 1024], P('depth', None, 'rows'), may hold values from -6 to 6
- phase_index: bfloat16 [8, 1024, 1024], P('depth', 'rows'), may hold values from -2 to 2
- absorption: bfloat16 [8, 1024, 1024], P('depth', 'rows'), may hold values from 0.099609375 to 2
Outputs:
- exits: float32 [4, 2, 1024, 1024], P('depth', None, 'rows')
All inputs are finite; a program needn't handle non-finite values.
Results may differ from a plain program's by a relative error of at most 0.0003.
Values may be sent and summed in bfloat16 or wider, within the bound.
No kernel may reach another device: no remote copies, remote signals or barrier semaphores. Data moves between devices by JAX's collectives and lax.ppermute only.
A program may use at most 64 MiB of HBM per device.

v0:
```python
import functools
import math

import jax
import jax.numpy as jnp
import ml_dtypes
import numpy as np
from jax import lax
from jax.experimental import pallas as pl
from jax.experimental.pallas import tpu as pltpu
from jax.sharding import PartitionSpec as P

TAYLOR = 4
LATERAL = 0.22
CONTRAST = 0.2
LANES = 128
VMEM_BYTES = 48 * 1024 * 1024
F32 = jnp.float32
BF16 = jnp.bfloat16


def gap_tables(length):
    frequency = np.arange(length)
    frequency = np.where(frequency < length // 2, frequency, frequency - length)
    response = np.exp(-1j * math.pi * (frequency * frequency % (8 * length)) / (4 * length))
    spread = np.fft.ifft(response)
    half = length // 2
    lag = np.arange(half)[:, None] - np.arange(half)[None, :]
    near, far = spread[lag % length], spread[(lag + half) % length]
    even, odd = (near + far) / 2, (near - far) / 2
    table = np.stack([even.real, even.imag, odd.real, odd.imag]).astype(np.float32)
    high = table.astype(ml_dtypes.bfloat16)
    low = (table - high.astype(np.float32)).astype(ml_dtypes.bfloat16)
    return np.stack([high, low])


def split(values):
    high = values.astype(BF16)
    return high, (values - high.astype(F32)).astype(BF16)


def product(tables, which, operand, transposed):
    high, low = operand

    def dot(part, data):
        table = tables[part, which]
        if transposed:
            return lax.dot_general(table, data, (((1,), (1,)), ((), ())), preferred_element_type=F32)
        return lax.dot_general(data, table, (((1,), (0,)), ((), ())), preferred_element_type=F32)

    return dot(0, high) + (dot(1, high) + dot(0, low))


def half_gap(tables, first, stacked, rows, transposed):
    operand = split(stacked)
    by_re = product(tables, first, operand, transposed)
    by_im = product(tables, first + 1, operand, transposed)
    if transposed:
        return (by_re[:, :rows] - by_im[:, rows:], by_re[:, rows:] + by_im[:, :rows])
    return (by_re[:rows] - by_im[rows:], by_re[rows:] + by_im[:rows])


def gap_transposed(tables, field, rows):
    half = field.shape[1] // 2
    left, right = field[:, :half], field[:, half:]
    even = half_gap(tables, 0, left + right, rows, True)
    odd = half_gap(tables, 2, left - right, rows, True)
    return [(even[0] + odd[0], even[1] + odd[1]), (even[0] - odd[0], even[1] - odd[1])]


def gap_from_blocks(tables, blocks_ref, rows):
    count = blocks_ref.shape[0] // 2

    def folded(sign):
        def part(lane):
            return jnp.concatenate(
                [
                    blocks_ref[i, :, lane : lane + LANES]
                    + sign * blocks_ref[i + count, :, lane : lane + LANES]
                    for i in range(count)
                ],
                axis=1,
            )

        return jnp.concatenate([part(0), part(LANES)], axis=0)

    even = half_gap(tables, 0, folded(1.0), rows, False)
    odd = half_gap(tables, 2, folded(-1.0), rows, False)
    return [(even[0] + odd[0], even[1] + odd[1]), (even[0] - odd[0], even[1] - odd[1])]


def apply_slices(count, inside, load_coefficients, bufs, phase, loss, length):
    tall = phase.shape[0]
    groups = tall // 8
    base = bufs[0]

    def step(source, target, weight, keep_halo):
        def group(index, flag=None):
            row = index * 8
            if not isinstance(index, int):
                row = pl.multiple_of(row, 8)
            mid = pl.ds(row + 8, 8)
            here = pl.ds(row, 8)
            gather, centre = [], []
            for part in range(2):
                cell = source[part, mid, :]
                width = cell.shape[1]
                around = source.at[part, pl.ds(row, 24)]
                total = (
                    around[7:15, :length]
                    + around[9:17, :length]
                    + pltpu.roll(cell, 1, 1)[:, :length]
                    + pltpu.roll(cell, width - 1, 1)[:, :length]
                )
                cell = cell[:, :length]
                gather.append(total + phase[here, :] * cell)
                centre.append(cell)
            damp = loss[here, :]
            new_re = base[0, mid, :length] - weight * (gather[1] + damp * centre[0])
            new_im = base[1, mid, :length] + weight * (gather[0] - damp * centre[1])
            if flag is not None:
                new_re = jnp.where(flag, new_re, 0.0)
                new_im = jnp.where(flag, new_im, 0.0)
            target[0, mid, :length] = new_re
            target[1, mid, :length] = new_im

        if keep_halo:
            group(0, inside[0])
            group(groups - 1, inside[1])

        def body(index, carry):
            group(index)
            return carry

        lax.fori_loop(1, groups - 1, body, 0)

    for slice_index in range(count):
        load_coefficients(slice_index)
        source = bufs[0]
        for degree in range(TAYLOR, 0, -1):
            target = bufs[0] if degree == 1 else bufs[1 + degree % 2]
            last = slice_index == count - 1 and degree == 1
            step(source, target, LATERAL / degree, not last)
            source = target


def scaled_phase(values):
    return values.astype(F32) * (CONTRAST / LATERAL) - 4.0


def scaled_loss(values):
    return values.astype(F32) * (CONTRAST / LATERAL)


def clear_margins(bufs, length):
    for buf in bufs:
        buf[:, :, length:] = jnp.zeros(buf.shape[:2] + (buf.shape[2] - length,), F32)


def first_kernel(
    height, count, width, edge_ref, field, above, below, index_ref, loss_ref, tables, out,
    buf0, buf1, buf2, phase, loss, spectrum,
):
    bufs = (buf0, buf1, buf2)
    length = field.shape[2]
    clear_margins(bufs, length)
    buf0[:, 8 : 8 + width, :length] = above[0:2]
    buf0[:, 8 + width : 8 + width + height, :length] = field[...]
    buf0[:, 8 + width + height : 8 + 2 * width + height, :length] = below[0:2]

    def load_coefficients(k):
        phase[0:width, :] = scaled_phase(above[2 + k])
        loss[0:width, :] = scaled_loss(above[2 + count + k])
        for row in range(0, height, 16):
            phase[width + row : width + row + 16, :] = scaled_phase(index_ref[k, row : row + 16, :])
            loss[width + row : width + row + 16, :] = scaled_loss(loss_ref[k, row : row + 16, :])
        phase[width + height :, :] = scaled_phase(below[2 + k])
        loss[width + height :, :] = scaled_loss(below[2 + count + k])

    inside = (edge_ref[0] > 0, edge_ref[1] > 0)
    apply_slices(count, inside, load_coefficients, bufs, phase, loss, length)
    core = buf0[:, 8 + width : 8 + width + height, :length]
    halves = gap_transposed(tables, core.reshape(2 * height, length), height)
    half = length // 2
    spectrum[0:width, :] = jnp.zeros((width, 2 * height), F32)
    spectrum[width + length :, :] = jnp.zeros((width, 2 * height), F32)
    for which, (real, imag) in enumerate(halves):
        start = width + which * half
        spectrum[start : start + half, :height] = real
        spectrum[start : start + half, height:] = imag
    for k in range(out.shape[0]):
        out[k] = spectrum[k * height : k * height + height + 2 * width, :]


def second_kernel(
    height, count, width, edge_ref, blocks, specimen, tables, out, buf0, buf1, buf2, phase, loss,
):
    bufs = (buf0, buf1, buf2)
    tall = height + 2 * width
    length = specimen.shape[2]
    half = length // 2
    clear_margins(bufs, length)
    for which, (real, imag) in enumerate(gap_from_blocks(tables, blocks, tall)):
        buf0[0, 8 : 8 + tall, which * half : (which + 1) * half] = real
        buf0[1, 8 : 8 + tall, which * half : (which + 1) * half] = imag

    def load_coefficients(k):
        for row in range(0, tall, 16):
            phase[row : row + 16, :] = scaled_phase(specimen[k, row : row + 16, :])
            loss[row : row + 16, :] = scaled_loss(specimen[count + k, row : row + 16, :])

    inside = (edge_ref[0] > 0, edge_ref[1] > 0)
    apply_slices(count, inside, load_coefficients, bufs, phase, loss, length)
    core = buf0[:, 8 + width : 8 + width + height, :length]
    for which, (real, imag) in enumerate(
        gap_transposed(tables, core.reshape(2 * height, length), height)
    ):
        out[which * half : (which + 1) * half, :height] = real
        out[which * half : (which + 1) * half, height:] = imag


def third_kernel(height, blocks, tables, out):
    half = out.shape[2] // 2
    for which, (real, imag) in enumerate(gap_from_blocks(tables, blocks, height)):
        out[0, :, which * half : (which + 1) * half] = real
        out[1, :, which * half : (which + 1) * half] = imag


VMEM = pl.BlockSpec(memory_space=pltpu.VMEM)
SMEM = pl.BlockSpec(memory_space=pltpu.SMEM)


def call(kernel, in_specs, out_shape, scratch, name, flops, moved):
    return pl.pallas_call(
        kernel,
        in_specs=in_specs,
        out_specs=VMEM,
        out_shape=out_shape,
        scratch_shapes=scratch,
        compiler_params=pltpu.CompilerParams(vmem_limit_bytes=VMEM_BYTES),
        cost_estimate=pl.CostEstimate(flops=flops, bytes_accessed=moved, transcendentals=0),
        name=name,
    )


def in_lane_blocks(pieces):
    sources, rows, both = pieces.shape
    own = both // 2
    if own == LANES:
        return pieces
    joined = pieces.reshape(sources, rows, 2, own).transpose(1, 2, 0, 3)
    joined = joined.reshape(rows, 2, sources * own // LANES, LANES).transpose(2, 0, 1, 3)
    return joined.reshape(sources * own // LANES, rows, 2 * LANES)


def to_others(pieces):
    return lax.all_to_all(pieces, "rows", split_axis=0, concat_axis=0, tiled=True)


def local(in_flight, phase_index, absorption):
    field = in_flight[0]
    count, height, length = phase_index.shape
    slabs = lax.axis_size("rows")
    groups = lax.axis_size("depth")
    width = count * TAYLOR
    tall = height + 2 * width
    place = lax.axis_index("rows")
    edge = jnp.stack([(place > 0), (place < slabs - 1)]).astype(jnp.int32)
    tables = jnp.asarray(gap_tables(length))

    def lines(start):
        def cut(array):
            return lax.slice_in_dim(array, start, start + width, axis=1).astype(F32)

        return jnp.concatenate([cut(field), cut(phase_index), cut(absorption)], axis=0)

    down = [(i, i + 1) for i in range(slabs - 1)]
    up = [(i + 1, i) for i in range(slabs - 1)]
    above = lax.ppermute(lines(height - width), "rows", down)
    below = lax.ppermute(lines(0), "rows", up)

    turned = jnp.concatenate([phase_index, absorption], axis=0).transpose(0, 2, 1)
    turned = jnp.pad(turned, ((0, 0), (width, width), (0, 0)))
    turned = jnp.stack(
        [lax.slice_in_dim(turned, k * height, k * height + tall, axis=1) for k in range(slabs)]
    )
    turned = to_others(turned)
    specimen = turned.transpose(1, 2, 0, 3).reshape(2 * count, tall, length)

    buffer = pltpu.VMEM((2, tall + 16, length + LANES), F32)
    coefficient = pltpu.VMEM((tall, length), F32)
    slice_flops = 40 * count * TAYLOR * tall * length
    gap_flops = 24 * height * length * length // 2
    pieces = call(
        functools.partial(first_kernel, height, count, width),
        [SMEM] + [VMEM] * 6,
        jax.ShapeDtypeStruct((slabs, tall, 2 * height), F32),
        [buffer] * 3 + [coefficient] * 2 + [pltpu.VMEM((length + 2 * width, 2 * height), F32)],
        "slices_and_gap_rows",
        slice_flops + gap_flops,
        8 * 1024 * 1024,
    )(edge, field, above, below, phase_index, absorption, tables)

    pieces = lax.ppermute(pieces, "depth", [(g, (g + 1) % groups) for g in range(groups)])
    blocks = in_lane_blocks(to_others(pieces))

    pieces = call(
        functools.partial(second_kernel, height, count, width),
        [SMEM] + [VMEM] * 3,
        jax.ShapeDtypeStruct((length, 2 * height), F32),
        [buffer] * 3 + [coefficient] * 2,
        "gap_slices_gap_columns",
        slice_flops + 2 * gap_flops,
        8 * 1024 * 1024,
    )(edge, blocks, specimen, tables)

    blocks = in_lane_blocks(to_others(pieces.reshape(slabs, height, 2 * height)))

    field = call(
        functools.partial(third_kernel, height),
        [VMEM] * 2,
        jax.ShapeDtypeStruct((2, height, length), F32),
        [],
        "gap_rows",
        gap_flops,
        6 * 1024 * 1024,
    )(blocks, tables)
    return field[None]


def solution(mesh):
    placed = (P("depth", None, "rows", None), P("depth", "rows", None), P("depth", "rows", None))
    return jax.shard_map(
        local, mesh=mesh, in_specs=placed, out_specs=P("depth", None, "rows", None), check_vma=False
    )
```

profile of v0, /device:TPU:0, one launch (start us, length us, event | category | flops | bytes accessed | tf_op | source)
XLA Modules:
  0.0 132.4 jit_solution(18266296802716231334)
XLA Ops:
  0.0 0.0 copy-start.2
  0.0 0.9 fusion.10
  0.9 0.0 copy-start.1
  1.0 0.9 slice_convert_fusion
  1.8 0.7 pad_maximum_fusion.1
  2.5 1.3 collective-permute-start.1
  3.8 0.7 pad_maximum_fusion
  4.5 3.0 %collective-permute-start = (f32[6,8,1024]{2,1,0:T(8,128)}, f32[6,8,1024]{2,1,0:T(8,128)S(1)}, u32[]{:S(2)}, u32[]{:S(2)}) collective-permute-start(f32[6,8,1024]{2,1,0:T(8,128)} %pad_maximum_fusion), channel_id=1, source_target_pairs={{0,1},{1,2},{2,3},{3,4},{4,5},{5,6},{6,7},{8,9},{9,10},{10,11},{11... | collective-permute-start | bytes 589832 | tf_op jit(solution)/shard_map/ppermute | solution.py:279
  7.6 0.0 copy-done.2
  7.6 0.3 copy.6
  7.8 0.0 copy-done.1
  7.8 0.3 copy.7
  8.1 0.1 maximum_bitcast_fusion
  8.2 0.0 copy-start.3
  8.2 0.7 fusion.1
  8.9 0.7 fusion.9
  9.6 0.7 fusion.8
  10.2 0.7 fusion.7
  10.9 0.7 fusion.6
  11.6 0.1 add_convert_fusion.edge_ref
  11.7 0.7 fusion.5
  12.3 0.0 collective-permute-done.1.below
  12.3 0.0 collective-permute-done.above
  12.3 0.0 copy-done.3
  12.3 22.7 %slices_and_gap_rows.1 = f32[8,144,256]{2,1,0:T(8,128)S(1)} custom-call(s32[2]{0:T(128)S(1)} %add_convert_fusion.edge_ref, f32[2,128,1024]{2,1,0:T(8,128)S(1)} %bitcast.46, f32[6,8,1024]{2,1,0:T(8,128)S(1)} %collective-permute-done.above, f32[6,8,1024]{2,1,0:T(8,128)S(1)} %collective-permute-done.1.below, bf16[2,128,1024]{2,1,0:T(8,128)(2,1)S(1)} %copy-done.2, ...), custom_call_target="tpu_custom_call" | custom-call | flops 1657798656 | bytes 8388608 | tf_op jit(solution)/shard_map/slices_and_gap_rows/pallas_call | solution.py:294
  35.0 3.1 %collective-permute-start.2 = (f32[8,144,256]{2,1,0:T(8,128)S(1)}, f32[8,144,256]{2,1,0:T(8,128)}, u32[]{:S(2)}, u32[]{:S(2)}) collective-permute-start(f32[8,144,256]{2,1,0:T(8,128)S(1)} %slices_and_gap_rows.1), channel_id=1, source_target_pairs={{0,8},{8,16},{16,24},{24,0},{1,9},{9,17},{17,25},{25,1},{2,10},{10... | collective-permute-start | bytes 3538952 | tf_op jit(solution)/shard_map/ppermute | solution.py:304
  38.1 0.7 fusion.4
  38.8 0.7 fusion.3
  39.4 21.4 %all_to_all.15 = bf16[8,4,144,128]{3,2,1,0:T(8,128)(2,1)} all-to-all(bf16[8,4,144,128]{3,2,1,0:T(8,128)(2,1)} %fusion.3), channel_id=1, replica_groups=mesh['depth'=4,'rows'=8] {'rows'}, dimensions={0} | all-to-all | bytes 2359296 | tf_op jit(solution)/shard_map/all_to_all | solution.py:257
  60.9 5.9 %collective-permute-done.2 = f32[8,144,256]{2,1,0:T(8,128)} collective-permute-done((f32[8,144,256]{2,1,0:T(8,128)S(1)}, f32[8,144,256]{2,1,0:T(8,128)}, u32[]{:S(2)}, u32[]{:S(2)}) %collective-permute-start.2) | collective-permute-done | bytes 1179680 | tf_op jit(solution)/shard_map/ppermute | solution.py:304
  66.7 3.6 %all-to-all-start = ((f32[8,144,256]{2,1,0:T(8,128)}), f32[8,144,256]{2,1,0:T(8,128)S(1)}, u32[]{:S(2)}, u32[]{:S(2)}) async-start(f32[8,144,256]{2,1,0:T(8,128)} %collective-permute-done.2), calls=%async_computation | async-start | bytes 2359296 | tf_op jit(solution)/shard_map/all_to_all | solution.py:257
  70.3 1.4 %copy_bitcast_fusion.specimen = bf16[4,144,1024]{2,1,0:T(8,128)(2,1)S(1)} fusion(bf16[8,4,144,128]{3,2,1,0:T(8,128)(2,1)} %all_to_all.15), kind=kLoop, calls=%fused_computation | loop fusion | bytes 2359296 | tf_op jit(solution)/shard_map/reshape | solution.py:288
  71.7 15.3 %all-to-all-done.blocks = f32[8,144,256]{2,1,0:T(8,128)S(1)} async-done(((f32[8,144,256]{2,1,0:T(8,128)}), f32[8,144,256]{2,1,0:T(8,128)S(1)}, u32[]{:S(2)}, u32[]{:S(2)}) %all-to-all-start) | async-done | bytes 1179680 | tf_op jit(solution)/shard_map/all_to_all | solution.py:257
  87.1 0.0 copy-start
  87.1 24.7 %gap_slices_gap_columns.1 = f32[1024,256]{1,0:T(8,128)S(1)} custom-call(s32[2]{0:T(128)S(1)} %add_convert_fusion.edge_ref, f32[8,144,256]{2,1,0:T(8,128)S(1)} %all-to-all-done.blocks, bf16[4,144,1024]{2,1,0:T(8,128)(2,1)S(1)} %copy_bitcast_fusion.specimen, bf16[2,4,512,512]{3,2,1,0:T(8,128)(2,1)} %constant.12.clone.tables), custom_call_target="tpu_custom_call" | custom-call | flops 3268411392 | bytes 8388608 | tf_op jit(solution)/shard_map/gap_slices_gap_columns/pallas_call | solution.py:307
  111.8 17.8 %all_to_all.16.blocks = f32[8,128,256]{2,1,0:T(8,128)S(1)} all-to-all(f32[8,128,256]{2,1,0:T(8,128)S(1)} %bitcast.47), channel_id=1, replica_groups=mesh['depth'=4,'rows'=8] {'rows'}, dimensions={0} | all-to-all | bytes 2097152 | tf_op jit(solution)/shard_map/all_to_all | solution.py:257
  129.6 0.0 copy-done
  129.6 2.8 %gap_rows.1 = f32[2,128,1024]{2,1,0:T(8,128)} custom-call(f32[8,128,256]{2,1,0:T(8,128)S(1)} %all_to_all.16.blocks, bf16[2,4,512,512]{3,2,1,0:T(8,128)(2,1)S(1)} %copy-done), custom_call_target="tpu_custom_call" | custom-call | flops 1610612736 | bytes 6291456 | tf_op jit(solution)/shard_map/gap_rows/pallas_call | solution.py:319
Async XLA Ops:
  0.0 7.6 %copy-start.2 = (bf16[2,128,1024]{2,1,0:T(8,128)(2,1)S(1)}, bf16[2,128,1024]{2,1,0:T(8,128)(2,1)}, u32[]{:S(2)}) copy-start(bf16[2,128,1024]{2,1,0:T(8,128)(2,1)} %index_ref.1) | copy-start | bytes 1572868
  0.9 6.9 %copy-start.1 = (bf16[2,128,1024]{2,1,0:T(8,128)(2,1)S(1)}, bf16[2,128,1024]{2,1,0:T(8,128)(2,1)}, u32[]{:S(2)}) copy-start(bf16[2,128,1024]{2,1,0:T(8,128)(2,1)} %loss_ref.1) | copy-start | bytes 1572868
  2.5 9.8 %collective-permute-start.1 = (f32[6,8,1024]{2,1,0:T(8,128)}, f32[6,8,1024]{2,1,0:T(8,128)S(1)}, u32[]{:S(2)}, u32[]{:S(2)}) collective-permute-start(f32[6,8,1024]{2,1,0:T(8,128)} %pad_maximum_fusion.1), channel_id=1, source_target_pairs={{1,0},{2,1},{3,2},{4,3},{5,4},{6,5},{7,6},{9,8},{10,9},{11,10},{12... | collective-permute-start | bytes 589832 | tf_op jit(solution)/shard_map/ppermute | solution.py:280
  4.5 7.8 %collective-permute-start = (f32[6,8,1024]{2,1,0:T(8,128)}, f32[6,8,1024]{2,1,0:T(8,128)S(1)}, u32[]{:S(2)}, u32[]{:S(2)}) collective-permute-start(f32[6,8,1024]{2,1,0:T(8,128)} %pad_maximum_fusion), channel_id=1, source_target_pairs={{0,1},{1,2},{2,3},{3,4},{4,5},{5,6},{6,7},{8,9},{9,10},{10,11},{11... | collective-permute-start | bytes 589832 | tf_op jit(solution)/shard_map/ppermute | solution.py:279
  8.2 4.1 %copy-start.3 = (f32[1,2,128,1024]{3,2,1,0:T(8,128)S(1)}, f32[1,2,128,1024]{3,2,1,0:T(8,128)}, u32[]{:S(2)}) copy-start(f32[1,2,128,1024]{3,2,1,0:T(8,128)} %param.4) | copy-start | bytes 3145732
  35.0 31.7 %collective-permute-start.2 = (f32[8,144,256]{2,1,0:T(8,128)S(1)}, f32[8,144,256]{2,1,0:T(8,128)}, u32[]{:S(2)}, u32[]{:S(2)}) collective-permute-start(f32[8,144,256]{2,1,0:T(8,128)S(1)} %slices_and_gap_rows.1), channel_id=1, source_target_pairs={{0,8},{8,16},{16,24},{24,0},{1,9},{9,17},{17,25},{25,1},{2,10},{10... | collective-permute-start | bytes 3538952 | tf_op jit(solution)/shard_map/ppermute | solution.py:304
  66.7 20.4 %all-to-all-start = ((f32[8,144,256]{2,1,0:T(8,128)}), f32[8,144,256]{2,1,0:T(8,128)S(1)}, u32[]{:S(2)}, u32[]{:S(2)}) async-start(f32[8,144,256]{2,1,0:T(8,128)} %collective-permute-done.2), calls=%async_computation | async-start | bytes 2359296 | tf_op jit(solution)/shard_map/all_to_all | solution.py:257
  87.1 42.5 %copy-start = (bf16[2,4,512,512]{3,2,1,0:T(8,128)(2,1)S(1)}, bf16[2,4,512,512]{3,2,1,0:T(8,128)(2,1)}, u32[]{:S(2)}) copy-start(bf16[2,4,512,512]{3,2,1,0:T(8,128)(2,1)} %constant.12.clone.tables) | copy-start | bytes 12582916
where the time goes:
time: 133 us; the launch traced here: 132 us
  Pallas kernels  50.2 us (38%)
  blocking collectives  39.2 us (29%)
  waiting for transfers between devices  21.2 us (16%)
  starting transfers between devices  11 us (8%)
  local copies, waits for them, and re-layouts  8.29 us (6%)
  other arithmetic  2.43 us (2%)
    all_to_all x2, blocking collectives, to_others(): lax.all_to_all(pieces, 'rows', split_axis=0, concat_axis=0, tiled=True)  39.2 us
    pallas_call x1, Pallas kernels, local(): call(functools.partial(second_kernel, height, count, width), [SMEM] + [VM...  24.7 us
    pallas_call x1, Pallas kernels, local(): call(functools.partial(first_kernel, height, count, width), [SMEM] + [VME...  22.7 us
    all_to_all x1, waiting for transfers between devices, to_others(): lax.all_to_all(pieces, 'rows', split_axis=0, concat_axis=0, tiled=True)  15.3 us
    ppermute x1, waiting for transfers between devices, local(): lax.ppermute(pieces, 'depth', [(g, (g + 1) % groups) for g in range(group...  5.88 us
    unnamed x17, local copies, waits for them, and re-layouts  5.25 us
    all_to_all x1, starting transfers between devices, to_others(): lax.all_to_all(pieces, 'rows', split_axis=0, concat_axis=0, tiled=True)  3.56 us
    ppermute x1, starting transfers between devices, local(): lax.ppermute(pieces, 'depth', [(g, (g + 1) % groups) for g in range(group...  3.08 us
  transfers between devices with their start and end apart: 4, of which 2 were waited for; matrix products, arithmetic and copies ran while one was open for 6% of the time, Pallas kernels for 0%

commit v1 on v0

v1 whole, which is shorter than its diff:
```python
import functools
import math

import jax
import jax.numpy as jnp
import ml_dtypes
import numpy as np
from jax import lax
from jax.experimental import pallas as pl
from jax.experimental.pallas import tpu as pltpu
from jax.sharding import PartitionSpec as P

TAYLOR = 4
LATERAL = 0.22
CONTRAST = 0.2
LANES = 128
VMEM_BYTES = 48 * 1024 * 1024
F32 = jnp.float32
BF16 = jnp.bfloat16


def gap_tables(length):
    frequency = np.arange(length)
    frequency = np.where(frequency < length // 2, frequency, frequency - length)
    response = np.exp(-1j * math.pi * (frequency * frequency % (8 * length)) / (4 * length))
    spread = np.fft.ifft(response)
    half = length // 2
    lag = np.arange(half)[:, None] - np.arange(half)[None, :]
    near, far = spread[lag % length], spread[(lag + half) % length]
    even, odd = (near + far) / 2, (near - far) / 2
    table = np.stack([even.real, even.imag, odd.real, odd.imag]).astype(np.float32)
    high = table.astype(ml_dtypes.bfloat16)
    low = (table - high.astype(np.float32)).astype(ml_dtypes.bfloat16)
    return np.stack([high, low])


FLOOR = 255.0
SPAN = 250.0
STEEP = SPAN / math.log2(1.0 + FLOOR)
SCALE_ROWS = 16


def scale_of(arrays):
    largest = functools.reduce(jnp.maximum, [jnp.max(jnp.abs(array)) for array in arrays])
    return jnp.maximum(largest * (1.0 + 2.0**-7), 1e-30).astype(BF16).astype(F32)


def encode(values, scale):
    level = jnp.log2(1.0 + jnp.abs(values) * (FLOOR / scale))
    code = jnp.exp2(level * STEEP - SPAN / 2)
    return jnp.where(values < 0, -code, code).astype(BF16)


def decode(codes, scale):
    codes = codes.astype(F32)
    level = (jnp.log2(jnp.abs(codes)) + SPAN / 2) * (1.0 / STEEP)
    values = (jnp.exp2(level) - 1.0) * (scale * (1.0 / FLOOR))
    return jnp.where(codes < 0, -values, values)


def decode_block(blocks_ref, i, lane, rows):
    lanes = slice(lane, lane + LANES)
    scale = blocks_ref[i, rows : rows + SCALE_ROWS, lanes].astype(F32)[0:1]
    return decode(blocks_ref[i, 0:rows, lanes], scale)


def split(values):
    high = values.astype(BF16)
    return high, (values - high.astype(F32)).astype(BF16)


def product(tables, which, operand, transposed):
    high, low = operand

    def dot(part, data):
        table = tables[part, which]
        if transposed:
            return lax.dot_general(table, data, (((1,), (1,)), ((), ())), preferred_element_type=F32)
        return lax.dot_general(data, table, (((1,), (0,)), ((), ())), preferred_element_type=F32)

    return dot(0, high) + (dot(1, high) + dot(0, low))


def half_gap(tables, first, stacked, rows, transposed):
    operand = split(stacked)
    by_re = product(tables, first, operand, transposed)
    by_im = product(tables, first + 1, operand, transposed)
    if transposed:
        return (by_re[:, :rows] - by_im[:, rows:], by_re[:, rows:] + by_im[:, :rows])
    return (by_re[:rows] - by_im[rows:], by_re[rows:] + by_im[:rows])


def gap_transposed(tables, field, rows):
    half = field.shape[1] // 2
    left, right = field[:, :half], field[:, half:]
    even = half_gap(tables, 0, left + right, rows, True)
    odd = half_gap(tables, 2, left - right, rows, True)
    return [(even[0] + odd[0], even[1] + odd[1]), (even[0] - odd[0], even[1] - odd[1])]


def gap_from_blocks(tables, blocks_ref, rows):
    count = blocks_ref.shape[0] // 2

    parts = [
        [decode_block(blocks_ref, i, lane, rows) for i in range(2 * count)] for lane in (0, LANES)
    ]

    def folded(sign):
        return jnp.concatenate(
            [
                jnp.concatenate([part[i] + sign * part[i + count] for i in range(count)], axis=1)
                for part in parts
            ],
            axis=0,
        )

    even = half_gap(tables, 0, folded(1.0), rows, False)
    odd = half_gap(tables, 2, folded(-1.0), rows, False)
    return [(even[0] + odd[0], even[1] + odd[1]), (even[0] - odd[0], even[1] - odd[1])]


def shifted(row):
    lane = lax.broadcasted_iota(jnp.int32, row[0].shape, 1)
    count = len(row)
    right = [pltpu.roll(cell, 1, 1) for cell in row]
    left = [pltpu.roll(cell, LANES - 1, 1) for cell in row]
    before = [
        jnp.where(lane == 0, right[i - 1] if i else 0.0, right[i]) for i in range(count)
    ]
    after = [
        jnp.where(lane == LANES - 1, left[i + 1] if i + 1 < count else 0.0, left[i])
        for i in range(count)
    ]
    return before, after


def spread_rows(natural, target, first):
    blocks, tall, _ = natural.shape
    steps = tall // 8
    for i in range(blocks):
        for k in range(steps):
            target[i, 8 * (k + first) : 8 * (k + first) + 8, :] = natural.at[i][
                pl.ds(k, 8, stride=steps), :
            ]


def gather_rows(source, first, natural):
    blocks, tall, _ = natural.shape
    steps = tall // 8
    for i in range(blocks):
        for k in range(steps):
            natural.at[i][pl.ds(k, 8, stride=steps), :] = source[
                i, 8 * (k + first) : 8 * (k + first) + 8, :
            ]


def wrap(buf, steps):
    for part in range(2):
        for i in range(buf.shape[1]):
            last = buf[part, i, 8 * steps : 8 * steps + 8, :]
            buf[part, i, 0:8, :] = pltpu.roll(last, 1, 0)
            initial = buf[part, i, 8:16, :]
            buf[part, i, 8 * steps + 8 : 8 * steps + 16, :] = pltpu.roll(initial, 7, 0)


def apply_slices(count, width, inside, load_coefficients, bufs, phase, loss, keep):
    blocks, tall, _ = phase.shape
    steps = tall // 8
    sublane = lax.broadcasted_iota(jnp.int32, (8, LANES), 0)
    for k in range(steps if inside else 0):
        row = sublane * steps + k
        top = jnp.logical_and(row < width, inside[0] == 0)
        bottom = jnp.logical_and(row >= tall - width, inside[1] == 0)
        keep[8 * k : 8 * k + 8, :] = jnp.where(jnp.logical_or(top, bottom), 0.0, 1.0)
    base = bufs[0]

    def step(source, target, weight):
        def body(k):
            def rows(ref, at, *lead):
                start = (k + at) * 8
                return [ref[lead + (i, pl.ds(start, 8), slice(None))] for i in range(blocks)]

            factor = keep[pl.ds(k * 8, 8), :] * weight if inside else weight
            phases = rows(phase, 0)
            losses = rows(loss, 0)
            here, total = [], []
            for part in range(2):
                cells = rows(source, 1, part)
                above, below = rows(source, 0, part), rows(source, 2, part)
                before, after = shifted(cells)
                here.append(cells)
                total.append(
                    [
                        (above[i] + below[i]) + (before[i] + after[i]) + phases[i] * cells[i]
                        for i in range(blocks)
                    ]
                )
            start = pl.ds((k + 1) * 8, 8)
            for i in range(blocks):
                target[0, i, start, :] = base[0, i, start, :] - factor * (
                    total[1][i] + losses[i] * here[0][i]
                )
                target[1, i, start, :] = base[1, i, start, :] + factor * (
                    total[0][i] - losses[i] * here[1][i]
                )

        for k in range(steps):
            body(k)
        wrap(target, steps)

    def one_slice(slice_index, carry):
        load_coefficients(slice_index)
        source = bufs[0]
        for degree in range(TAYLOR, 0, -1):
            target = bufs[0] if degree == 1 else bufs[1 + degree % 2]
            step(source, target, LATERAL / degree)
            source = target
        return carry

    lax.fori_loop(0, count, one_slice, 0)


def scaled_phase(values):
    return values.astype(F32) * (CONTRAST / LATERAL) - 4.0


def scaled_loss(values):
    return values.astype(F32) * (CONTRAST / LATERAL)


def by_blocks(target, start, values):
    rows = values.shape[0]
    for i in range(values.shape[1] // LANES):
        target[i, start : start + rows, :] = values[:, i * LANES : (i + 1) * LANES]


def joined(natural, start, rows):
    return jnp.concatenate(
        [
            jnp.concatenate(
                [natural[part, i, start : start + rows, :] for i in range(natural.shape[1])], axis=1
            )
            for part in range(2)
        ],
        axis=0,
    )


def lines_kernel(
    height, count, width, field, index_ref, loss_ref, head, tail, cells, deltas, absorbs, sems
):
    copies = []
    for end, start in enumerate((0, height - width)):
        copies.append((field.at[:, pl.ds(start, width)], cells.at[end]))
    for end, start in enumerate((0, height - 16)):
        copies.append((index_ref.at[:, pl.ds(start, 16)], deltas.at[end]))
        copies.append((loss_ref.at[:, pl.ds(start, 16)], absorbs.at[end]))
    started = [
        pltpu.make_async_copy(source, target, sems.at[i])
        for i, (source, target) in enumerate(copies)
    ]
    for copy in started:
        copy.start()
    for copy in started:
        copy.wait()
    for end, out in enumerate((head, tail)):
        out[0:2] = cells[end]
        skip = 0 if end == 0 else 16 - width
        for k in range(count):
            out[2 + k] = deltas[end, k].astype(F32)[skip : skip + width]
            out[2 + count + k] = absorbs[end, k].astype(F32)[skip : skip + width]


def turn_kernel(height, count, width, index_ref, loss_ref, out, turned):
    length = index_ref.shape[2]
    side = 2 * LANES
    diagonal = lax.broadcasted_iota(jnp.int32, (side, side), 0) == lax.broadcasted_iota(
        jnp.int32, (side, side), 1
    )
    identity = jnp.where(diagonal, 1.0, 0.0).astype(BF16)
    margin = jnp.zeros((width, height), F32)
    for which, source in enumerate((index_ref, loss_ref)):
        for k in range(count):
            line = which * count + k
            turned[line, 0:width, :] = margin
            turned[line, width + length :, :] = margin
            for start in range(0, length, side):
                turned[line, width + start : width + start + side, :] = lax.dot_general(
                    identity,
                    source[k, :, start : start + side],
                    (((1,), (1,)), ((), ())),
                    preferred_element_type=F32,
                )
    for k in range(out.shape[0]):
        for line in range(2 * count):
            out[k, line] = turned[line, k * height : k * height + height + 2 * width, :].astype(BF16)


def put_coded(out, first, natural, rows, scale):
    start, stop = rows
    for i in range(natural.shape[0]):
        out[first : first + stop - start, i * LANES : (i + 1) * LANES] = encode(
            natural[i, start:stop, :], scale
        )


def put_scale(out, first, scale):
    out[first : first + SCALE_ROWS, :] = jnp.broadcast_to(
        scale, (SCALE_ROWS, out.shape[1])
    ).astype(BF16)


def inner_kernel(
    height, count, width, field, index_ref, loss_ref, out,
    buf0, buf1, buf2, phase, loss, keep, natural,
):
    bufs = (buf0, buf1, buf2)
    for part in range(2):
        for row in range(0, height, 16):
            by_blocks(natural.at[part], row, field[part, row : row + 16, :])
        spread_rows(natural.at[part], buf0.at[part], 1)
    wrap(buf0, height // 8)

    def load_coefficients(k):
        for which, (source, scale, target) in enumerate(
            ((index_ref, scaled_phase, phase), (loss_ref, scaled_loss, loss))
        ):
            for row in range(0, height, 16):
                by_blocks(natural.at[which], row, scale(source[k, row : row + 16, :]))
            spread_rows(natural.at[which], target, 0)

    apply_slices(count, width, None, load_coefficients, bufs, phase, loss, keep)
    for part in range(2):
        gather_rows(buf0.at[part], 1, natural.at[part])
    rows = (width, height - width)
    inner = height - 2 * width
    scale = scale_of([natural[part, :, width : height - width, :] for part in range(2)])
    for part in range(2):
        put_coded(out, part * inner, natural.at[part], rows, scale)
    put_scale(out, 2 * inner, scale)


def outer_kernel(
    height, count, width, edge_ref, field, above, below, index_ref, loss_ref, out,
    buf0, buf1, buf2, phase, loss, keep, natural,
):
    bufs = (buf0, buf1, buf2)
    own = 2 * width
    tall = 6 * width

    def place(target, line, ends):
        by_blocks(target, 0, above[line].astype(F32))
        by_blocks(target, width, ends[0].astype(F32))
        by_blocks(target, width + own, ends[1].astype(F32))
        by_blocks(target, width + 2 * own, below[line].astype(F32))

    for part in range(2):
        place(natural.at[part], part, (field[part, 0:own, :], field[part, height - own :, :]))
        spread_rows(natural.at[part], buf0.at[part], 1)
    wrap(buf0, tall // 8)

    def load_coefficients(k):
        for which, (source, scale, target) in enumerate(
            ((index_ref, scaled_phase, phase), (loss_ref, scaled_loss, loss))
        ):
            line = 2 + which * count + k
            place(natural.at[which], line, (source[k, 0:own, :], source[k, height - own :, :]))
            for i in range(natural.shape[1]):
                natural[which, i] = scale(natural[which, i])
            spread_rows(natural.at[which], target, 0)

    inside = (edge_ref[0], edge_ref[1])
    apply_slices(count, width, inside, load_coefficients, bufs, phase, loss, keep)
    for part in range(2):
        gather_rows(buf0.at[part], 1, natural.at[part])
    ends = ((width, 2 * width), (4 * width, 5 * width))
    scale = scale_of([natural[part, :, s:e, :] for part in range(2) for s, e in ends])
    for part in range(2):
        for i in range(natural.shape[1]):
            both = jnp.concatenate([natural[part, i, s:e, :] for s, e in ends], axis=0)
            out[part * own : (part + 1) * own, i * LANES : (i + 1) * LANES] = encode(both, scale)
    put_scale(out, 2 * own, scale)


def rows_kernel(height, width, inner_ref, outer_ref, tables, out, field, spectrum):
    length = inner_ref.shape[1]
    inner = height - 2 * width

    def scale_in(ref, row):
        return ref[row : row + SCALE_ROWS, :].astype(F32)[0:1]

    inner_scale = scale_in(inner_ref, 2 * inner)
    outer_scale = scale_in(outer_ref, 4 * width)
    for part in range(2):
        start = part * height
        ends = decode(outer_ref[2 * part * width : 2 * (part + 1) * width, :], outer_scale)
        field[start : start + width, :] = ends[:width]
        field[start + height - width : start + height, :] = ends[width:]
        for row in range(0, inner, 16):
            field[start + width + row : start + width + row + 16, :] = decode(
                inner_ref[part * inner + row : part * inner + row + 16, :], inner_scale
            )
    halves = gap_transposed(tables, field[...], height)
    half = length // 2
    spectrum[0:width, :] = jnp.zeros((width, 2 * height), F32)
    spectrum[width + length :, :] = jnp.zeros((width, 2 * height), F32)
    for which, (real, imag) in enumerate(halves):
        start = width + which * half
        spectrum[start : start + half, :height] = real
        spectrum[start : start + half, height:] = imag
    scale = scale_of([part for pair in halves for part in pair])
    tall = height + 2 * width
    for k in range(out.shape[0]):
        out[k, 0:tall, :] = encode(spectrum[k * height : k * height + tall, :], scale)
        put_scale(out.at[k], tall, scale)


def second_kernel(
    height, count, width, edge_ref, blocks, specimen, tables, out,
    buf0, buf1, buf2, phase, loss, keep, natural,
):
    bufs = (buf0, buf1, buf2)
    tall = height + 2 * width
    length = out.shape[0] * height
    half = length // 2
    for which, halves in enumerate(gap_from_blocks(tables, blocks, tall)):
        for part in range(2):
            by_blocks(natural.at[part, pl.ds(which * half // LANES, half // LANES)], 0, halves[part])
    inside = (edge_ref[0], edge_ref[1])
    for part in range(2):
        for i in range(natural.shape[1]):
            for end, rows in enumerate((slice(0, width), slice(tall - width, tall))):
                line = natural[part, i, rows, :]
                natural[part, i, rows, :] = jnp.where(inside[end] > 0, line, 0.0)
        spread_rows(natural.at[part], buf0.at[part], 1)
    wrap(buf0, tall // 8)

    def load_coefficients(k):
        for which, (scale, target) in enumerate(((scaled_phase, phase), (scaled_loss, loss))):
            for i in range(specimen.shape[0]):
                for row in range(0, tall, 16):
                    natural[which, i, row : row + 16, :] = scale(
                        specimen[i, which * count + k, row : row + 16, :]
                    )
            spread_rows(natural.at[which], target, 0)

    apply_slices(count, width, inside, load_coefficients, bufs, phase, loss, keep)
    for part in range(2):
        gather_rows(buf0.at[part], 1, natural.at[part])
    halves = gap_transposed(tables, joined(natural, width, height), height)
    scale = scale_of([part for pair in halves for part in pair])
    rows_of_half = out.shape[0] // 2
    for which, (real, imag) in enumerate(halves):
        for k in range(rows_of_half):
            rows = slice(k * height, (k + 1) * height)
            target = which * rows_of_half + k
            out[target, 0:height, :height] = encode(real[rows], scale)
            out[target, 0:height, height:] = encode(imag[rows], scale)
            out[target, height:, :] = jnp.broadcast_to(scale, (SCALE_ROWS, 2 * height)).astype(BF16)


def third_kernel(height, blocks, tables, out):
    half = out.shape[2] // 2
    for which, (real, imag) in enumerate(gap_from_blocks(tables, blocks, height)):
        out[0, :, which * half : (which + 1) * half] = real
        out[1, :, which * half : (which + 1) * half] = imag


VMEM = pl.BlockSpec(memory_space=pltpu.VMEM)
SMEM = pl.BlockSpec(memory_space=pltpu.SMEM)
HBM = pl.BlockSpec(memory_space=pltpu.HBM)


def call(kernel, in_specs, out_shape, scratch, name, flops, moved, outs=1):
    return pl.pallas_call(
        kernel,
        in_specs=in_specs,
        out_specs=VMEM if outs == 1 else (VMEM,) * outs,
        out_shape=out_shape,
        scratch_shapes=scratch,
        compiler_params=pltpu.CompilerParams(vmem_limit_bytes=VMEM_BYTES),
        cost_estimate=pl.CostEstimate(flops=flops, bytes_accessed=moved, transcendentals=0),
        name=name,
    )


def in_lane_blocks(pieces):
    sources, rows, both = pieces.shape
    own = both // 2
    if own == LANES:
        return pieces
    joined = pieces.reshape(sources, rows, 2, own).transpose(1, 2, 0, 3)
    joined = joined.reshape(rows, 2, sources * own // LANES, LANES).transpose(2, 0, 1, 3)
    return joined.reshape(sources * own // LANES, rows, 2 * LANES)


def to_others(pieces):
    return lax.all_to_all(pieces, "rows", split_axis=0, concat_axis=0, tiled=True)


def local(in_flight, phase_index, absorption):
    field = in_flight[0]
    count, height, length = phase_index.shape
    slabs = lax.axis_size("rows")
    groups = lax.axis_size("depth")
    width = count * TAYLOR
    tall = height + 2 * width
    place = lax.axis_index("rows")
    edge = jnp.stack([(place > 0), (place < slabs - 1)]).astype(jnp.int32)
    tables = jnp.asarray(gap_tables(length))

    lane_blocks = length // LANES

    def working(rows):
        buffer = pltpu.VMEM((2, lane_blocks, rows + 16, LANES), F32)
        coefficient = pltpu.VMEM((lane_blocks, rows, LANES), F32)
        return [buffer] * 3 + [coefficient] * 2 + [
            pltpu.VMEM((rows, LANES), F32),
            pltpu.VMEM((2, lane_blocks, rows, LANES), F32),
        ]

    def slice_cost(rows):
        cells = count * TAYLOR * rows * length
        return 40 * cells, 32 * cells

    gap_flops = 24 * height * length * length // 2
    to_next = [(g, (g + 1) % groups) for g in range(groups)]

    turned = call(
        functools.partial(turn_kernel, height, count, width),
        [VMEM] * 2,
        jax.ShapeDtypeStruct((slabs, 2 * count, tall, height), BF16),
        [pltpu.VMEM((2 * count, length + 2 * width, height), F32)],
        "specimen_columns",
        0,
        0,
    )(phase_index, absorption)
    turned, field = lax.optimization_barrier((turned, field))
    specimen = to_others(turned)

    inner = call(
        functools.partial(inner_kernel, height, count, width),
        [VMEM] * 3,
        jax.ShapeDtypeStruct((2 * (height - 2 * width) + SCALE_ROWS, length), BF16),
        working(height),
        "slices_inner_rows",
        *slice_cost(height),
    )(field, phase_index, absorption)
    inner, late_field = lax.optimization_barrier((inner, field))
    inner = lax.ppermute(inner, "depth", to_next)

    line_shape = jax.ShapeDtypeStruct((2 + 2 * count, width, length), F32)
    head, tail = call(
        functools.partial(lines_kernel, height, count, width),
        [HBM] * 3,
        (line_shape, line_shape),
        [
            pltpu.VMEM((2, 2, width, length), F32),
            pltpu.VMEM((2, count, 16, length), BF16),
            pltpu.VMEM((2, count, 16, length), BF16),
            pltpu.SemaphoreType.DMA((6,)),
        ],
        "edge_lines",
        0,
        0,
        2,
    )(late_field, phase_index, absorption)
    down = [(i, i + 1) for i in range(slabs - 1)]
    up = [(i + 1, i) for i in range(slabs - 1)]
    above = lax.ppermute(tail, "rows", down)
    below = lax.ppermute(head, "rows", up)
    outer = call(
        functools.partial(outer_kernel, height, count, width),
        [SMEM] + [VMEM] * 5,
        jax.ShapeDtypeStruct((4 * width + SCALE_ROWS, length), BF16),
        working(6 * width),
        "slices_outer_rows",
        0,
        0,
    )(edge, late_field, above, below, phase_index, absorption)

    outer = lax.ppermute(outer, "depth", to_next)
    if height != LANES:
        specimen = specimen.transpose(1, 2, 0, 3).reshape(2 * count, tall, -1, LANES)
        specimen = specimen.transpose(2, 0, 1, 3)

    pieces = call(
        functools.partial(rows_kernel, height, width),
        [VMEM] * 3,
        jax.ShapeDtypeStruct((slabs, tall + SCALE_ROWS, 2 * height), BF16),
        [
            pltpu.VMEM((2 * height, length), F32),
            pltpu.VMEM((length + 2 * width, 2 * height), F32),
        ],
        "gap_along_rows",
        gap_flops,
        8 * 1024 * 1024,
    )(inner, outer, tables)
    pieces, specimen = lax.optimization_barrier((pieces, specimen))
    blocks = in_lane_blocks(to_others(pieces))

    pieces = call(
        functools.partial(second_kernel, height, count, width),
        [SMEM] + [VMEM] * 3,
        jax.ShapeDtypeStruct((slabs, height + SCALE_ROWS, 2 * height), BF16),
        working(tall),
        "gap_slices_gap_columns",
        *slice_cost(tall),
    )(edge, blocks, specimen, tables)

    blocks = in_lane_blocks(to_others(pieces))

    field = call(
        functools.partial(third_kernel, height),
        [VMEM] * 2,
        jax.ShapeDtypeStruct((2, height, length), F32),
        [],
        "gap_rows",
        gap_flops,
        6 * 1024 * 1024,
    )(blocks, tables)
    return field[None]


def solution(mesh):
    placed = (P("depth", None, "rows", None), P("depth", "rows", None), P("depth", "rows", None))
    return jax.shard_map(
        local, mesh=mesh, in_specs=placed, out_specs=P("depth", None, "rows", None), check_vma=False
    )
```

time: 133 us -> 90.1 us (0.68)
  Pallas kernels: 50.2 us -> 34 us
  waiting for transfers between devices: 21.2 us -> 8.55 us
  blocking collectives: 39.2 us -> 30.7 us
  local copies, waits for them, and re-layouts: 8.29 us -> 4.29 us
  other arithmetic: 2.43 us -> 0.08 us
    all_to_all x1, waiting for transfers between devices: 15.3 us -> 0.01 us  [to_others(): lax.all_to_all(pieces, 'rows', split_axis=0, concat_axis=0, tiled=True)]
    pallas_call x1, Pallas kernels: 24.7 us -> 13.4 us  [local(): call(functools.partial(second_kernel, height, count, width), [SMEM] + [VM...]
    all_to_all x2, blocking collectives: 39.2 us -> 30.7 us  [to_others(): lax.all_to_all(pieces, 'rows', split_axis=0, concat_axis=0, tiled=True)]
    pallas_call x1 -> x5, Pallas kernels: 22.7 us -> 17.4 us  [the longest x1 7.66 us: local(): call(functools.partial(inner_kernel, height, count, width), [VMEM] * 3, j...]
    ppermute x3 -> x4, waiting for transfers between devices: 5.89 us -> 8.54 us  [the longest x1 4.84 us: local(): outer = lax.ppermute(outer, 'depth', to_next)]
    all_to_all x1, starting transfers between devices: 3.56 us -> 5.3 us  [to_others(): lax.all_to_all(pieces, 'rows', split_axis=0, concat_axis=0, tiled=True)]
    reshape x1 -> x0, local copies, waits for them, and re-layouts: 1.44 us -> none  [local(): specimen = turned.transpose(1, 2, 0, 3).reshape(2 * count, tall, length)]
    concatenate x2 -> x0, other arithmetic: 1.38 us -> none  [lines(): jnp.concatenate([cut(field), cut(phase_index), cut(absorption)], axis=0)]
  transfers between devices with their start and end apart: 4 -> 5, of which waited for: 2 -> 2; matrix products, arithmetic and copies ran while one was open for 6% -> 0% of each run, Pallas kernels for 0% -> 17%
where the time goes in v1:
time: 90.1 us; the launch traced here: 89.6 us
  Pallas kernels  34 us (38%)
  blocking collectives  30.7 us (34%)
  starting transfers between devices  11.9 us (13%)
  waiting for transfers between devices  8.55 us (9%)
  local copies, waits for them, and re-layouts  4.29 us (5%)
    all_to_all x2, blocking collectives, to_others(): lax.all_to_all(pieces, 'rows', split_axis=0, concat_axis=0, tiled=True)  30.7 us
    pallas_call x1, Pallas kernels, local(): call(functools.partial(second_kernel, height, count, width), [SMEM] + [VM...  13.4 us
    pallas_call x1, Pallas kernels, local(): call(functools.partial(inner_kernel, height, count, width), [VMEM] * 3, j...  7.66 us
    all_to_all x1, starting transfers between devices, to_others(): lax.all_to_all(pieces, 'rows', split_axis=0, concat_axis=0, tiled=True)  5.3 us
    ppermute x1, waiting for transfers between devices, local(): outer = lax.ppermute(outer, 'depth', to_next)  4.84 us
    unnamed x14, local copies, waits for them, and re-layouts  4.29 us
    pallas_call x1, Pallas kernels, local(): call(functools.partial(rows_kernel, height, width), [VMEM] * 3, jax.Shape...  3.7 us
    ppermute x1, waiting for transfers between devices, local(): below = lax.ppermute(head, 'rows', up)  3.7 us
  transfers between devices with their start and end apart: 5, of which 2 were waited for; matrix products, arithmetic and copies ran while one was open for 0% of the time, Pallas kernels for 17%

profile of v1, /device:TPU:0, one launch (start us, length us, event | category | flops | bytes accessed | tf_op | source)
XLA Modules:
  0.0 89.6 jit_solution(1029321563502475151)
XLA Ops:
  0.0 0.0 copy-start.1
  0.0 1.0 %copy-done.1 = bf16[2,128,1024]{2,1,0:T(8,128)(2,1)S(1)} copy-done((bf16[2,128,1024]{2,1,0:T(8,128)(2,1)S(1)}, bf16[2,128,1024]{2,1,0:T(8,128)(2,1)}, u32[]{:S(2)}) %copy-start.1) | copy-done | bytes 524312
  1.0 0.0 copy-start.3
  1.0 1.0 %copy-done.3 = bf16[2,128,1024]{2,1,0:T(8,128)(2,1)S(1)} copy-done((bf16[2,128,1024]{2,1,0:T(8,128)(2,1)S(1)}, bf16[2,128,1024]{2,1,0:T(8,128)(2,1)}, u32[]{:S(2)}) %copy-start.3) | copy-done | bytes 524312
  2.1 1.7 %specimen_columns.1 = bf16[8,4,144,128]{3,2,1,0:T(8,128)(2,1)} custom-call(bf16[2,128,1024]{2,1,0:T(8,128)(2,1)S(1)} %copy-done.1, bf16[2,128,1024]{2,1,0:T(8,128)(2,1)S(1)} %copy-done.3), custom_call_target="tpu_custom_call" | custom-call | tf_op jit(solution)/shard_map/specimen_columns/pallas_call | solution.py:529
  3.8 0.0 copy-start
  3.8 0.0 copy-start.2
  3.8 0.0 copy-start.4
  3.8 5.3 %all-to-all-start = ((bf16[8,4,144,128]{3,2,1,0:T(8,128)(2,1)}), bf16[8,4,144,128]{3,2,1,0:T(8,128)(2,1)S(1)}, u32[]{:S(2)}, u32[]{:S(2)}) async-start(bf16[8,4,144,128]{3,2,1,0:T(8,128)(2,1)} %specimen_columns.1), calls=%async_computation | async-start | bytes 2359296 | tf_op jit(solution)/shard_map/all_to_all | solution.py:498
  9.1 0.0 copy-done
  9.1 0.0 copy-done.2
  9.1 0.0 copy-done.4
  9.2 7.7 %slices_inner_rows.1 = bf16[240,1024]{1,0:T(8,128)(2,1)} custom-call(f32[2,128,1024]{2,1,0:T(8,128)S(1)} %bitcast.4, bf16[2,128,1024]{2,1,0:T(8,128)(2,1)S(1)} %copy-done.2, bf16[2,128,1024]{2,1,0:T(8,128)(2,1)S(1)} %copy-done.4), custom_call_target="tpu_custom_call" | custom-call | flops 41943040 | bytes 33554432 | tf_op jit(solution)/shard_map/slices_inner_rows/pallas_call | solution.py:541
  16.8 1.6 %collective-permute-start = (bf16[240,1024]{1,0:T(8,128)(2,1)}, bf16[240,1024]{1,0:T(8,128)(2,1)}, u32[]{:S(2)}, u32[]{:S(2)}) collective-permute-start(bf16[240,1024]{1,0:T(8,128)(2,1)} %slices_inner_rows.1), channel_id=1, source_target_pairs={{0,8},{8,16},{16,24},{24,0},{1,9},{9,17},{17,25},{25,1},{2,10},{10... | collective-permute-start | bytes 1474568 | tf_op jit(solution)/shard_map/ppermute | solution.py:550
  18.4 1.1 %edge_lines.1 = (f32[6,8,1024]{2,1,0:T(8,128)}, f32[6,8,1024]{2,1,0:T(8,128)}) custom-call(f32[2,128,1024]{2,1,0:T(8,128)S(1)} %bitcast.5, bf16[2,128,1024]{2,1,0:T(8,128)(2,1)S(1)} %copy-done.2, bf16[2,128,1024]{2,1,0:T(8,128)(2,1)S(1)} %copy-done.4), custom_call_target="tpu_custom_call" | custom-call | tf_op jit(solution)/shard_map/edge_lines/pallas_call | solution.py:553
  19.5 2.1 %collective-permute-start.1 = (f32[6,8,1024]{2,1,0:T(8,128)}, f32[6,8,1024]{2,1,0:T(8,128)S(1)}, u32[]{:S(2)}, u32[]{:S(2)}) collective-permute-start(f32[6,8,1024]{2,1,0:T(8,128)} %get-tuple-element.16), channel_id=1, source_target_pairs={{0,1},{1,2},{2,3},{3,4},{4,5},{5,6},{6,7},{8,9},{9,10},{10,11},{11... | collective-permute-start | bytes 589832 | tf_op jit(solution)/shard_map/ppermute | solution.py:570
  21.6 1.3 %collective-permute-start.2 = (f32[6,8,1024]{2,1,0:T(8,128)}, f32[6,8,1024]{2,1,0:T(8,128)}, u32[]{:S(2)}, u32[]{:S(2)}) collective-permute-start(f32[6,8,1024]{2,1,0:T(8,128)} %get-tuple-element.17), channel_id=1, source_target_pairs={{1,0},{2,1},{3,2},{4,3},{5,4},{6,5},{7,6},{9,8},{10,9},{11,10},{12... | collective-permute-start | bytes 589832 | tf_op jit(solution)/shard_map/ppermute | solution.py:571
  22.9 0.1 add_convert_fusion.edge_ref
  23.0 0.0 collective-permute-done.1.above
  23.0 3.7 %collective-permute-done.2.below = f32[6,8,1024]{2,1,0:T(8,128)} collective-permute-done((f32[6,8,1024]{2,1,0:T(8,128)}, f32[6,8,1024]{2,1,0:T(8,128)}, u32[]{:S(2)}, u32[]{:S(2)}) %collective-permute-start.2) | collective-permute-done | bytes 196640 | tf_op jit(solution)/shard_map/ppermute | solution.py:571
  26.7 3.2 %slices_outer_rows.1 = bf16[48,1024]{1,0:T(8,128)(2,1)S(1)} custom-call(s32[2]{0:T(128)S(1)} %add_convert_fusion.edge_ref, f32[2,128,1024]{2,1,0:T(8,128)S(1)} %bitcast.6, f32[6,8,1024]{2,1,0:T(8,128)S(1)} %collective-permute-done.1.above, f32[6,8,1024]{2,1,0:T(8,128)} %collective-permute-done.2.below, bf16[2,128,1024]{2,1,0:T(8,128)(2,1)S(1)} %copy-done.2, ...), custom_call_target="tpu_custom_call" | custom-call | tf_op jit(solution)/shard_map/slices_outer_rows/pallas_call | solution.py:572
  29.9 1.6 %collective-permute-start.3 = (bf16[48,1024]{1,0:T(8,128)(2,1)S(1)}, bf16[48,1024]{1,0:T(8,128)(2,1)S(1)}, u32[]{:S(2)}, u32[]{:S(2)}) collective-permute-start(bf16[48,1024]{1,0:T(8,128)(2,1)S(1)} %slices_outer_rows.1), channel_id=1, source_target_pairs={{0,8},{8,16},{16,24},{24,0},{1,9},{9,17},{17,25},{25,1},{2,10},{10... | collective-permute-start | bytes 294920 | tf_op jit(solution)/shard_map/ppermute | solution.py:582
  31.6 4.8 %collective-permute-done.3.outer_ref = bf16[48,1024]{1,0:T(8,128)(2,1)S(1)} collective-permute-done((bf16[48,1024]{1,0:T(8,128)(2,1)S(1)}, bf16[48,1024]{1,0:T(8,128)(2,1)S(1)}, u32[]{:S(2)}, u32[]{:S(2)}) %collective-permute-start.3) | collective-permute-done | bytes 98336 | tf_op jit(solution)/shard_map/ppermute | solution.py:582
  36.4 0.0 collective-permute-done.inner_ref
  36.4 0.0 copy-start.5
  36.4 2.2 %copy-done.5 = bf16[2,4,512,512]{3,2,1,0:T(8,128)(2,1)S(1)} copy-done((bf16[2,4,512,512]{3,2,1,0:T(8,128)(2,1)S(1)}, bf16[2,4,512,512]{3,2,1,0:T(8,128)(2,1)}, u32[]{:S(2)}) %copy-start.5) | copy-done | bytes 4194328
  38.6 3.7 %gap_along_rows.1 = bf16[8,160,256]{2,1,0:T(8,128)(2,1)S(1)} custom-call(bf16[240,1024]{1,0:T(8,128)(2,1)} %collective-permute-done.inner_ref, bf16[48,1024]{1,0:T(8,128)(2,1)S(1)} %collective-permute-done.3.outer_ref, bf16[2,4,512,512]{3,2,1,0:T(8,128)(2,1)S(1)} %copy-done.5), custom_call_target="tpu_custom_call" | custom-call | flops 1610612736 | bytes 8388608 | tf_op jit(solution)/shard_map/gap_along_rows/pallas_call | solution.py:587
  42.3 0.0 all-to-all-done.specimen
  42.3 17.9 %all_to_all.15.blocks = bf16[8,160,256]{2,1,0:T(8,128)(2,1)S(1)} all-to-all(bf16[8,160,256]{2,1,0:T(8,128)(2,1)S(1)} %gap_along_rows.1), channel_id=1, replica_groups=mesh['depth'=4,'rows'=8] {'rows'}, dimensions={0} | all-to-all | bytes 1310720 | tf_op jit(solution)/shard_map/all_to_all | solution.py:498
  60.2 0.0 copy-start.6
  60.2 13.4 %gap_slices_gap_columns.1 = bf16[8,144,256]{2,1,0:T(8,128)(2,1)S(1)} custom-call(s32[2]{0:T(128)S(1)} %add_convert_fusion.edge_ref, bf16[8,160,256]{2,1,0:T(8,128)(2,1)S(1)} %all_to_all.15.blocks, bf16[8,4,144,128]{3,2,1,0:T(8,128)(2,1)S(1)} %all-to-all-done.specimen, bf16[2,4,512,512]{3,2,1,0:T(8,128)(2,1)} %constant.10.clone.tables), custom_call_target="tpu_custom_call" | custom-call | flops 47185920 | bytes 37748736 | tf_op jit(solution)/shard_map/gap_slices_gap_columns/pallas_call | solution.py:602
  73.6 12.8 %all_to_all.16.blocks = bf16[8,144,256]{2,1,0:T(8,128)(2,1)S(1)} all-to-all(bf16[8,144,256]{2,1,0:T(8,128)(2,1)S(1)} %gap_slices_gap_columns.1), channel_id=1, replica_groups=mesh['depth'=4,'rows'=8] {'rows'}, dimensions={0} | all-to-all | bytes 1179648 | tf_op jit(solution)/shard_map/all_to_all | solution.py:498
  86.5 0.0 copy-done.6
  86.5 3.1 %gap_rows.1 = f32[2,128,1024]{2,1,0:T(8,128)} custom-call(bf16[8,144,256]{2,1,0:T(8,128)(2,1)S(1)} %all_to_all.16.blocks, bf16[2,4,512,512]{3,2,1,0:T(8,128)(2,1)S(1)} %copy-done.6), custom_call_target="tpu_custom_call" | custom-call | flops 1610612736 | bytes 6291456 | tf_op jit(solution)/shard_map/gap_rows/pallas_call | solution.py:613
Async XLA Ops:
  0.0 1.0 %copy-start.1 = (bf16[2,128,1024]{2,1,0:T(8,128)(2,1)S(1)}, bf16[2,128,1024]{2,1,0:T(8,128)(2,1)}, u32[]{:S(2)}) copy-start(bf16[2,128,1024]{2,1,0:T(8,128)(2,1)} %index_ref.7) | copy-start | bytes 1572868
  1.0 1.0 %copy-start.3 = (bf16[2,128,1024]{2,1,0:T(8,128)(2,1)S(1)}, bf16[2,128,1024]{2,1,0:T(8,128)(2,1)}, u32[]{:S(2)}) copy-start(bf16[2,128,1024]{2,1,0:T(8,128)(2,1)} %loss_ref.7) | copy-start | bytes 1572868
  3.8 5.3 %copy-start = (f32[1,2,128,1024]{3,2,1,0:T(8,128)S(1)}, f32[1,2,128,1024]{3,2,1,0:T(8,128)}, u32[]{:S(2)}) copy-start(f32[1,2,128,1024]{3,2,1,0:T(8,128)} %param.4) | copy-start | bytes 3145732
  3.8 5.3 %copy-start.2 = (bf16[2,128,1024]{2,1,0:T(8,128)(2,1)S(1)}, bf16[2,128,1024]{2,1,0:T(8,128)(2,1)}, u32[]{:S(2)}) copy-start(bf16[2,128,1024]{2,1,0:T(8,128)(2,1)} %index_ref.7) | copy-start | bytes 1572868
  3.8 5.3 %copy-start.4 = (bf16[2,128,1024]{2,1,0:T(8,128)(2,1)S(1)}, bf16[2,128,1024]{2,1,0:T(8,128)(2,1)}, u32[]{:S(2)}) copy-start(bf16[2,128,1024]{2,1,0:T(8,128)(2,1)} %loss_ref.7) | copy-start | bytes 1572868
  3.8 38.5 %all-to-all-start = ((bf16[8,4,144,128]{3,2,1,0:T(8,128)(2,1)}), bf16[8,4,144,128]{3,2,1,0:T(8,128)(2,1)S(1)}, u32[]{:S(2)}, u32[]{:S(2)}) async-start(bf16[8,4,144,128]{3,2,1,0:T(8,128)(2,1)} %specimen_columns.1), calls=%async_computation | async-start | bytes 2359296 | tf_op jit(solution)/shard_map/all_to_all | solution.py:498
  16.8 19.6 %collective-permute-start = (bf16[240,1024]{1,0:T(8,128)(2,1)}, bf16[240,1024]{1,0:T(8,128)(2,1)}, u32[]{:S(2)}, u32[]{:S(2)}) collective-permute-start(bf16[240,1024]{1,0:T(8,128)(2,1)} %slices_inner_rows.1), channel_id=1, source_target_pairs={{0,8},{8,16},{16,24},{24,0},{1,9},{9,17},{17,25},{25,1},{2,10},{10... | collective-permute-start | bytes 1474568 | tf_op jit(solution)/shard_map/ppermute | solution.py:550
  19.5 3.5 %collective-permute-start.1 = (f32[6,8,1024]{2,1,0:T(8,128)}, f32[6,8,1024]{2,1,0:T(8,128)S(1)}, u32[]{:S(2)}, u32[]{:S(2)}) collective-permute-start(f32[6,8,1024]{2,1,0:T(8,128)} %get-tuple-element.16), channel_id=1, source_target_pairs={{0,1},{1,2},{2,3},{3,4},{4,5},{5,6},{6,7},{8,9},{9,10},{10,11},{11... | collective-permute-start | bytes 589832 | tf_op jit(solution)/shard_map/ppermute | solution.py:570
  21.6 5.1 %collective-permute-start.2 = (f32[6,8,1024]{2,1,0:T(8,128)}, f32[6,8,1024]{2,1,0:T(8,128)}, u32[]{:S(2)}, u32[]{:S(2)}) collective-permute-start(f32[6,8,1024]{2,1,0:T(8,128)} %get-tuple-element.17), channel_id=1, source_target_pairs={{1,0},{2,1},{3,2},{4,3},{5,4},{6,5},{7,6},{9,8},{10,9},{11,10},{12... | collective-permute-start | bytes 589832 | tf_op jit(solution)/shard_map/ppermute | solution.py:571
  29.9 6.5 %collective-permute-start.3 = (bf16[48,1024]{1,0:T(8,128)(2,1)S(1)}, bf16[48,1024]{1,0:T(8,128)(2,1)S(1)}, u32[]{:S(2)}, u32[]{:S(2)}) collective-permute-start(bf16[48,1024]{1,0:T(8,128)(2,1)S(1)} %slices_outer_rows.1), channel_id=1, source_target_pairs={{0,8},{8,16},{16,24},{24,0},{1,9},{9,17},{17,25},{25,1},{2,10},{10... | collective-permute-start | bytes 294920 | tf_op jit(solution)/shard_map/ppermute | solution.py:582
  36.4 2.2 %copy-start.5 = (bf16[2,4,512,512]{3,2,1,0:T(8,128)(2,1)S(1)}, bf16[2,4,512,512]{3,2,1,0:T(8,128)(2,1)}, u32[]{:S(2)}) copy-start(bf16[2,4,512,512]{3,2,1,0:T(8,128)(2,1)} %constant.10.clone.tables) | copy-start | bytes 12582916
  60.2 26.3 %copy-start.6 = (bf16[2,4,512,512]{3,2,1,0:T(8,128)(2,1)S(1)}, bf16[2,4,512,512]{3,2,1,0:T(8,128)(2,1)}, u32[]{:S(2)}) copy-start(bf16[2,4,512,512]{3,2,1,0:T(8,128)(2,1)} %constant.10.clone.tables) | copy-start | bytes 12582916

commit v2 on v1

--- a/solution.py
+++ b/solution.py
@@ -14,24 +14,39 @@
 LATERAL = 0.22
 CONTRAST = 0.2
 LANES = 128
-VMEM_BYTES = 48 * 1024 * 1024
+VMEM_BYTES = 24 * 1024 * 1024
+ALL_VMEM_BYTES = 60 * 1024 * 1024
 F32 = jnp.float32
 BF16 = jnp.bfloat16
 
 
-def gap_tables(length):
+def circulant_split(column):
+    length = column.shape[0]
+    half = length // 2
+    lag = np.arange(half)[:, None] - np.arange(half)[None, :]
+    near, far = column[lag % length], column[(lag + half) % length]
+    return (near + far) / 2, (near - far) / 2
+
+
+def interleave(length):
+    return np.arange(length).reshape(-1, LANES, 2).transpose(0, 2, 1).reshape(-1)
+
+
+def gap_tables(length, interleaved):
     frequency = np.arange(length)
     frequency = np.where(frequency < length // 2, frequency, frequency - length)
     response = np.exp(-1j * math.pi * (frequency * frequency % (8 * length)) / (4 * length))
-    spread = np.fft.ifft(response)
-    half = length // 2
-    lag = np.arange(half)[:, None] - np.arange(half)[None, :]
-    near, far = spread[lag % length], spread[(lag + half) % length]
-    even, odd = (near + far) / 2, (near - far) / 2
-    table = np.stack([even.real, even.imag, odd.real, odd.imag]).astype(np.float32)
-    high = table.astype(ml_dtypes.bfloat16)
-    low = (table - high.astype(np.float32)).astype(ml_dtypes.bfloat16)
-    return np.stack([high, low])
+    even, odd = circulant_split(np.fft.ifft(response))
+    parts = []
+    for blocks in (circulant_split(even[:, 0]), (odd,)):
+        table = np.stack([t for block in blocks for t in (block.real, block.imag)])
+        if interleaved:
+            table = table[:, :, interleave(table.shape[2])]
+        table = table.astype(np.float32)
+        high = table.astype(ml_dtypes.bfloat16)
+        low = (table - high.astype(np.float32)).astype(ml_dtypes.bfloat16)
+        parts.append(jnp.asarray(np.stack([high, low])))
+    return parts
 
 
 FLOOR = 255.0
@@ -90,12 +105,24 @@
     return (by_re[:rows] - by_im[rows:], by_re[rows:] + by_im[:rows])
 
 
+def gap_of_parts(tables, even, odd, rows, transposed):
+    small, large = tables
+    quarter = even.shape[1] // 2
+    left, right = even[:, :quarter], even[:, quarter:]
+    sums = half_gap(small, 0, left + right, rows, transposed)
+    differences = half_gap(small, 2, left - right, rows, transposed)
+    axis = 0 if transposed else 1
+    even = [
+        jnp.concatenate([x + y, x - y], axis=axis) for x, y in zip(sums, differences, strict=True)
+    ]
+    odd = half_gap(large, 0, odd, rows, transposed)
+    return [(even[0] + odd[0], even[1] + odd[1]), (even[0] - odd[0], even[1] - odd[1])]
+
+
 def gap_transposed(tables, field, rows):
     half = field.shape[1] // 2
     left, right = field[:, :half], field[:, half:]
-    even = half_gap(tables, 0, left + right, rows, True)
-    odd = half_gap(tables, 2, left - right, rows, True)
-    return [(even[0] + odd[0], even[1] + odd[1]), (even[0] - odd[0], even[1] - odd[1])]
+    return gap_of_parts(tables, left + right, left - right, rows, True)
 
 
 def gap_from_blocks(tables, blocks_ref, rows):
@@ -114,23 +141,20 @@
             axis=0,
         )
 
-    even = half_gap(tables, 0, folded(1.0), rows, False)
-    odd = half_gap(tables, 2, folded(-1.0), rows, False)
-    return [(even[0] + odd[0], even[1] + odd[1]), (even[0] - odd[0], even[1] - odd[1])]
+    return gap_of_parts(tables, folded(1.0), folded(-1.0), rows, False)
 
 
 def shifted(row):
     lane = lax.broadcasted_iota(jnp.int32, row[0].shape, 1)
     count = len(row)
-    right = [pltpu.roll(cell, 1, 1) for cell in row]
-    left = [pltpu.roll(cell, LANES - 1, 1) for cell in row]
-    before = [
-        jnp.where(lane == 0, right[i - 1] if i else 0.0, right[i]) for i in range(count)
-    ]
-    after = [
-        jnp.where(lane == LANES - 1, left[i + 1] if i + 1 < count else 0.0, left[i])
-        for i in range(count)
-    ]
+    moved_right = [pltpu.roll(row[i], 1, 1) for i in range(1, count, 2)]
+    moved_left = [pltpu.roll(row[i], LANES - 1, 1) for i in range(0, count, 2)]
+    before, after = [], []
+    for i in range(count // 2):
+        outside = moved_right[i - 1] if i else 0.0
+        before += [jnp.where(lane == 0, outside, moved_right[i]), row[2 * i]]
+        outside = moved_left[i + 1] if 2 * i + 2 < count else 0.0
+        after += [row[2 * i + 1], jnp.where(lane == LANES - 1, outside, moved_left[i])]
     return before, after
 
 
@@ -163,8 +187,8 @@
             buf[part, i, 8 * steps + 8 : 8 * steps + 16, :] = pltpu.roll(initial, 7, 0)
 
 
-def apply_slices(count, width, inside, load_coefficients, bufs, phase, loss, keep):
-    blocks, tall, _ = phase.shape
+def apply_slices(count, width, inside, bufs, phase, loss, keep):
+    _, blocks, tall, _ = phase.shape
     steps = tall // 8
     sublane = lax.broadcasted_iota(jnp.int32, (8, LANES), 0)
     for k in range(steps if inside else 0):
@@ -174,15 +198,15 @@
         keep[8 * k : 8 * k + 8, :] = jnp.where(jnp.logical_or(top, bottom), 0.0, 1.0)
     base = bufs[0]
 
-    def step(source, target, weight):
+    def step(slice_index, source, target, weight):
         def body(k):
             def rows(ref, at, *lead):
                 start = (k + at) * 8
                 return [ref[lead + (i, pl.ds(start, 8), slice(None))] for i in range(blocks)]
 
             factor = keep[pl.ds(k * 8, 8), :] * weight if inside else weight
-            phases = rows(phase, 0)
-            losses = rows(loss, 0)
+            phases = rows(phase, 0, slice_index)
+            losses = rows(loss, 0, slice_index)
             here, total = [], []
             for part in range(2):
                 cells = rows(source, 1, part)
@@ -209,11 +233,10 @@
         wrap(target, steps)
 
     def one_slice(slice_index, carry):
-        load_coefficients(slice_index)
         source = bufs[0]
         for degree in range(TAYLOR, 0, -1):
             target = bufs[0] if degree == 1 else bufs[1 + degree % 2]
-            step(source, target, LATERAL / degree)
+            step(slice_index, source, target, LATERAL / degree)
             source = target
         return carry
 
@@ -232,6 +255,57 @@
     rows = values.shape[0]
     for i in range(values.shape[1] // LANES):
         target[i, start : start + rows, :] = values[:, i * LANES : (i + 1) * LANES]
+
+
+def interleaving():
+    side = 2 * LANES
+    line = lax.broadcasted_iota(jnp.int32, (side, side), 0)
+    place = lax.broadcasted_iota(jnp.int32, (side, side), 1)
+    chosen = line == 2 * (place % LANES) + place // LANES
+    return jnp.where(chosen, 1.0, 0.0).astype(BF16)
+
+
+def interleaved(field, specimen):
+    order = interleaving()
+    side = 2 * LANES
+    rows = field.shape[0] if field is not None else 0
+    for first in range(0, specimen.shape[1], side):
+        parts = [specimen[:, first : first + side]]
+        if rows:
+            rest = field[:, first : first + side]
+            for _ in range(3):
+                part = rest.astype(BF16)
+                parts.append(part)
+                rest = rest - part.astype(F32)
+        lines = lax.dot_general(
+            jnp.concatenate(parts, axis=0) if rows else parts[0],
+            order,
+            (((1,), (0,)), ((), ())),
+            preferred_element_type=F32,
+        )
+        own = specimen.shape[0]
+        cells = None
+        if rows:
+            high, mid, low = (lines[own + i * rows : own + (i + 1) * rows] for i in range(3))
+            cells = high + (mid + low)
+        yield first // LANES, cells, lines[:own]
+
+
+def spread_interleaved(field, specimen, count, natural, buf, phase, loss):
+    rows = specimen.shape[0] // (2 * count)
+    for block, cells, lines in interleaved(field, specimen):
+        blocks = pl.ds(block, 2)
+        for part in range(2):
+            by_blocks(natural.at[part, blocks], 0, cells[part * rows : (part + 1) * rows])
+        for k in range(2 * count):
+            scale = scaled_phase if k < count else scaled_loss
+            by_blocks(natural.at[2 + k, blocks], 0, scale(lines[k * rows : (k + 1) * rows]))
+    for part in range(2):
+        spread_rows(natural.at[part], buf.at[part], 1)
+    wrap(buf, rows // 8)
+    for k in range(count):
+        spread_rows(natural.at[2 + k], phase.at[k], 0)
+        spread_rows(natural.at[2 + count + k], loss.at[k], 0)
 
 
 def joined(natural, start, rows):
@@ -315,21 +389,14 @@
     buf0, buf1, buf2, phase, loss, keep, natural,
 ):
     bufs = (buf0, buf1, buf2)
-    for part in range(2):
-        for row in range(0, height, 16):
-            by_blocks(natural.at[part], row, field[part, row : row + 16, :])
-        spread_rows(natural.at[part], buf0.at[part], 1)
-    wrap(buf0, height // 8)
-
-    def load_coefficients(k):
-        for which, (source, scale, target) in enumerate(
-            ((index_ref, scaled_phase, phase), (loss_ref, scaled_loss, loss))
-        ):
-            for row in range(0, height, 16):
-                by_blocks(natural.at[which], row, scale(source[k, row : row + 16, :]))
-            spread_rows(natural.at[which], target, 0)
-
-    apply_slices(count, width, None, load_coefficients, bufs, phase, loss, keep)
+    length = field.shape[2]
+    specimen = [ref[...].reshape(count * height, length) for ref in (index_ref, loss_ref)]
+    spread_interleaved(
+        field[...].reshape(2 * height, length),
+        jnp.concatenate(specimen, axis=0),
+        count, natural, buf0, phase, loss,
+    )
+    apply_slices(count, width, None, bufs, phase, loss, keep)
     for part in range(2):
         gather_rows(buf0.at[part], 1, natural.at[part])
     rows = (width, height - width)
@@ -341,36 +408,29 @@
 
 
 def outer_kernel(
-    height, count, width, edge_ref, field, above, below, index_ref, loss_ref, out,
+    height, count, width, edge_ref, field, above, below, index_ref, loss_ref, ready, out,
     buf0, buf1, buf2, phase, loss, keep, natural,
 ):
+    del ready
     bufs = (buf0, buf1, buf2)
     own = 2 * width
-    tall = 6 * width
-
-    def place(target, line, ends):
-        by_blocks(target, 0, above[line].astype(F32))
-        by_blocks(target, width, ends[0].astype(F32))
-        by_blocks(target, width + own, ends[1].astype(F32))
-        by_blocks(target, width + 2 * own, below[line].astype(F32))
-
-    for part in range(2):
-        place(natural.at[part], part, (field[part, 0:own, :], field[part, height - own :, :]))
-        spread_rows(natural.at[part], buf0.at[part], 1)
-    wrap(buf0, tall // 8)
-
-    def load_coefficients(k):
-        for which, (source, scale, target) in enumerate(
-            ((index_ref, scaled_phase, phase), (loss_ref, scaled_loss, loss))
-        ):
-            line = 2 + which * count + k
-            place(natural.at[which], line, (source[k, 0:own, :], source[k, height - own :, :]))
-            for i in range(natural.shape[1]):
-                natural[which, i] = scale(natural[which, i])
-            spread_rows(natural.at[which], target, 0)
-
+
+    def around(line, source, k):
+        lines = [above[line], source[k, 0:own, :], source[k, height - own :, :], below[line]]
+        return [part.astype(F32) for part in lines]
+
+    cells = around(0, field, 0) + around(1, field, 1)
+    specimen = []
+    for which, source in enumerate((index_ref, loss_ref)):
+        for k in range(count):
+            specimen += around(2 + which * count + k, source, k)
+    spread_interleaved(
+        jnp.concatenate(cells, axis=0),
+        jnp.concatenate(specimen, axis=0).astype(BF16),
+        count, natural, buf0, phase, loss,
+    )
     inside = (edge_ref[0], edge_ref[1])
-    apply_slices(count, width, inside, load_coefficients, bufs, phase, loss, keep)
+    apply_slices(count, width, inside, bufs, phase, loss, keep)
     for part in range(2):
         gather_rows(buf0.at[part], 1, natural.at[part])
     ends = ((width, 2 * width), (4 * width, 5 * width))
@@ -382,7 +442,10 @@
     put_scale(out, 2 * own, scale)
 
 
-def rows_kernel(height, width, inner_ref, outer_ref, tables, out, field, spectrum):
+def rows_kernel(
+    height, width, inner_ref, outer_ref, small, large, out, field, spectrum
+):
+    tables = (small, large)
     length = inner_ref.shape[1]
     inner = height - 2 * width
 
@@ -415,10 +478,25 @@
         put_scale(out.at[k], tall, scale)
 
 
+def coefficients_kernel(count, specimen, out, natural):
+    tall = natural.shape[2]
+    lines = jnp.concatenate(
+        [specimen[i].reshape(2 * count * tall, LANES) for i in range(specimen.shape[0])], axis=1
+    )
+    for block, _, cells in interleaved(None, lines):
+        for k in range(2 * count):
+            scale = scaled_phase if k < count else scaled_loss
+            part = scale(cells[k * tall : (k + 1) * tall])
+            by_blocks(natural.at[k, pl.ds(block, 2)], 0, part)
+    for k in range(2 * count):
+        spread_rows(natural.at[k], out.at[k // count, k % count], 0)
+
+
 def second_kernel(
-    height, count, width, edge_ref, blocks, specimen, tables, out,
-    buf0, buf1, buf2, phase, loss, keep, natural,
+    height, count, width, edge_ref, blocks, coefficients, small, large, out,
+    buf0, buf1, buf2, keep, natural,
 ):
+    tables = (small, large)
     bufs = (buf0, buf1, buf2)
     tall = height + 2 * width
     length = out.shape[0] * height
@@ -434,17 +512,7 @@
                 natural[part, i, rows, :] = jnp.where(inside[end] > 0, line, 0.0)
         spread_rows(natural.at[part], buf0.at[part], 1)
     wrap(buf0, tall // 8)
-
-    def load_coefficients(k):
-        for which, (scale, target) in enumerate(((scaled_phase, phase), (scaled_loss, loss))):
-            for i in range(specimen.shape[0]):
-                for row in range(0, tall, 16):
-                    natural[which, i, row : row + 16, :] = scale(
-                        specimen[i, which * count + k, row : row + 16, :]
-                    )
-            spread_rows(natural.at[which], target, 0)
-
-    apply_slices(count, width, inside, load_coefficients, bufs, phase, loss, keep)
+    apply_slices(count, width, inside, bufs, coefficients.at[0], coefficients.at[1], keep)
     for part in range(2):
         gather_rows(buf0.at[part], 1, natural.at[part])
     halves = gap_transposed(tables, joined(natural, width, height), height)
@@ -456,29 +524,30 @@
             target = which * rows_of_half + k
             out[target, 0:height, :height] = encode(real[rows], scale)
             out[target, 0:height, height:] = encode(imag[rows], scale)
-            out[target, height:, :] = jnp.broadcast_to(scale, (SCALE_ROWS, 2 * height)).astype(BF16)
-
-
-def third_kernel(height, blocks, tables, out):
+            put_scale(out.at[target], height, scale)
+
+
+def third_kernel(height, blocks, small, large, out):
     half = out.shape[2] // 2
-    for which, (real, imag) in enumerate(gap_from_blocks(tables, blocks, height)):
+    halves = gap_from_blocks((small, large), blocks, height)
+    for which, (real, imag) in enumerate(halves):
         out[0, :, which * half : (which + 1) * half] = real
         out[1, :, which * half : (which + 1) * half] = imag
 
 
 VMEM = pl.BlockSpec(memory_space=pltpu.VMEM)
 SMEM = pl.BlockSpec(memory_space=pltpu.SMEM)
-HBM = pl.BlockSpec(memory_space=pltpu.HBM)
-
-
-def call(kernel, in_specs, out_shape, scratch, name, flops, moved, outs=1):
+ANY = pl.BlockSpec(memory_space=pl.ANY)
+
+
+def call(kernel, in_specs, out_shape, scratch, name, flops, moved, outs=1, room=VMEM_BYTES):
     return pl.pallas_call(
         kernel,
         in_specs=in_specs,
         out_specs=VMEM if outs == 1 else (VMEM,) * outs,
         out_shape=out_shape,
         scratch_shapes=scratch,
-        compiler_params=pltpu.CompilerParams(vmem_limit_bytes=VMEM_BYTES),
+        compiler_params=pltpu.CompilerParams(vmem_limit_bytes=room),
         cost_estimate=pl.CostEstimate(flops=flops, bytes_accessed=moved, transcendentals=0),
         name=name,
     )
@@ -507,16 +576,18 @@
     tall = height + 2 * width
     place = lax.axis_index("rows")
     edge = jnp.stack([(place > 0), (place < slabs - 1)]).astype(jnp.int32)
-    tables = jnp.asarray(gap_tables(length))
+    tables = gap_tables(length, False)
+    tables_interleaved = gap_tables(length, True)
 
     lane_blocks = length // LANES
 
-    def working(rows):
+    def working(rows, specimen):
         buffer = pltpu.VMEM((2, lane_blocks, rows + 16, LANES), F32)
-        coefficient = pltpu.VMEM((lane_blocks, rows, LANES), F32)
-        return [buffer] * 3 + [coefficient] * 2 + [
+        coefficient = pltpu.VMEM((count, lane_blocks, rows, LANES), F32)
+        arrays = 2 + 2 * count if specimen else 2
+        return [buffer] * 3 + [coefficient] * (2 if specimen else 0) + [
             pltpu.VMEM((rows, LANES), F32),
-            pltpu.VMEM((2, lane_blocks, rows, LANES), F32),
+            pltpu.VMEM((arrays, lane_blocks, rows, LANES), F32),
         ]
 
     def slice_cost(rows):
@@ -534,6 +605,7 @@
         "specimen_columns",
         0,
         0,
+        room=ALL_VMEM_BYTES,
     )(phase_index, absorption)
     turned, field = lax.optimization_barrier((turned, field))
     specimen = to_others(turned)
@@ -542,7 +614,7 @@
         functools.partial(inner_kernel, height, count, width),
         [VMEM] * 3,
         jax.ShapeDtypeStruct((2 * (height - 2 * width) + SCALE_ROWS, length), BF16),
-        working(height),
+        working(height, True),
         "slices_inner_rows",
         *slice_cost(height),
     )(field, phase_index, absorption)
@@ -552,7 +624,7 @@
     line_shape = jax.ShapeDtypeStruct((2 + 2 * count, width, length), F32)
     head, tail = call(
         functools.partial(lines_kernel, height, count, width),
-        [HBM] * 3,
+        [ANY] * 3,
         (line_shape, line_shape),
         [
             pltpu.VMEM((2, 2, width, length), F32),
@@ -569,24 +641,33 @@
     up = [(i + 1, i) for i in range(slabs - 1)]
     above = lax.ppermute(tail, "rows", down)
     below = lax.ppermute(head, "rows", up)
-    outer = call(
-        functools.partial(outer_kernel, height, count, width),
-        [SMEM] + [VMEM] * 5,
-        jax.ShapeDtypeStruct((4 * width + SCALE_ROWS, length), BF16),
-        working(6 * width),
-        "slices_outer_rows",
-        0,
-        0,
-    )(edge, late_field, above, below, phase_index, absorption)
-
-    outer = lax.ppermute(outer, "depth", to_next)
     if height != LANES:
         specimen = specimen.transpose(1, 2, 0, 3).reshape(2 * count, tall, -1, LANES)
         specimen = specimen.transpose(2, 0, 1, 3)
+    coefficients = call(
+        functools.partial(coefficients_kernel, count),
+        [VMEM],
+        jax.ShapeDtypeStruct((2, count, lane_blocks, tall, LANES), F32),
+        [pltpu.VMEM((2 * count, lane_blocks, tall, LANES), F32)],
+        "coefficients",
+        0,
+        8 * 1024 * 1024,
+    )(specimen)
+
+    outer = call(
+        functools.partial(outer_kernel, height, count, width),
+        [SMEM] + [VMEM] * 5 + [ANY],
+        jax.ShapeDtypeStruct((4 * width + SCALE_ROWS, length), BF16),
+        working(6 * width, True),
+        "slices_outer_rows",
+        *slice_cost(6 * width),
+    )(edge, late_field, above, below, phase_index, absorption, coefficients)
+
+    outer = lax.ppermute(outer, "depth", to_next)
 
     pieces = call(
         functools.partial(rows_kernel, height, width),
-        [VMEM] * 3,
+        [VMEM] * 4,
         jax.ShapeDtypeStruct((slabs, tall + SCALE_ROWS, 2 * height), BF16),
         [
             pltpu.VMEM((2 * height, length), F32),
@@ -595,30 +676,29 @@
         "gap_along_rows",
         gap_flops,
         8 * 1024 * 1024,
-    )(inner, outer, tables)
-    pieces, specimen = lax.optimization_barrier((pieces, specimen))
+    )(inner, outer, *tables_interleaved)
     blocks = in_lane_blocks(to_others(pieces))
 
     pieces = call(
         functools.partial(second_kernel, height, count, width),
-        [SMEM] + [VMEM] * 3,
+        [SMEM] + [VMEM] * 4,
         jax.ShapeDtypeStruct((slabs, height + SCALE_ROWS, 2 * height), BF16),
-        working(tall),
+        working(tall, False),
         "gap_slices_gap_columns",
         *slice_cost(tall),
-    )(edge, blocks, specimen, tables)
+    )(edge, blocks, coefficients, *tables_interleaved)
 
     blocks = in_lane_blocks(to_others(pieces))
 
     field = call(
         functools.partial(third_kernel, height),
-        [VMEM] * 2,
+        [VMEM] * 3,
         jax.ShapeDtypeStruct((2, height, length), F32),
         [],
         "gap_rows",
         gap_flops,
         6 * 1024 * 1024,
-    )(blocks, tables)
+    )(blocks, *tables)
     return field[None]
 
 

time: 90.1 us -> 80.8 us (0.90)
  local copies, waits for them, and re-layouts: 4.29 us -> 0.03 us
  Pallas kernels: 34 us -> 30 us
    pallas_call x1, Pallas kernels: 13.4 us -> 9.14 us  [local(): call(functools.partial(second_kernel, height, count, width), [SMEM] + [VM...]
    unnamed x14, local copies, waits for them, and re-layouts: 4.29 us -> 0.03 us
    all_to_all x1, waiting for transfers between devices: 0.01 us -> 3.82 us  [to_others(): lax.all_to_all(pieces, 'rows', split_axis=0, concat_axis=0, tiled=True)]
    ppermute x1, waiting for transfers between devices: 3.7 us -> 0.01 us  [local(): below = lax.ppermute(head, 'rows', up)]
    pallas_call x1, Pallas kernels: 1.74 us -> 3.09 us  [local(): call(functools.partial(turn_kernel, height, count, width), [VMEM] * 2, ja...]
    all_to_all x2, blocking collectives: 30.7 us -> 29.8 us  [to_others(): lax.all_to_all(pieces, 'rows', split_axis=0, concat_axis=0, tiled=True)]
    pallas_call x3 -> x4, Pallas kernels: 7.91 us -> 7.85 us  [the longest x1 3.41 us: local(): call(functools.partial(rows_kernel, height, width), [VMEM] * 4, jax.Shape...]
  transfers between devices with their start and end apart: 5 -> 5, of which waited for: 2 -> 3; matrix products, arithmetic and copies ran while one was open for 0% -> 0% of each run, Pallas kernels for 17% -> 14%
where the time goes in v2:
time: 80.8 us; the launch traced here: 80.5 us
  Pallas kernels  30 us (37%)
  blocking collectives  29.8 us (37%)
  starting transfers between devices  11.8 us (15%)
  waiting for transfers between devices  8.66 us (11%)
    all_to_all x2, blocking collectives, to_others(): lax.all_to_all(pieces, 'rows', split_axis=0, concat_axis=0, tiled=True)  29.8 us
    pallas_call x1, Pallas kernels, local(): call(functools.partial(second_kernel, height, count, width), [SMEM] + [VM...  9.14 us
    pallas_call x1, Pallas kernels, local(): call(functools.partial(inner_kernel, height, count, width), [VMEM] * 3, j...  6.8 us
    all_to_all x1, starting transfers between devices, to_others(): lax.all_to_all(pieces, 'rows', split_axis=0, concat_axis=0, tiled=True)  5.17 us
    ppermute x1, waiting for transfers between devices, local(): outer = lax.ppermute(outer, 'depth', to_next)  4.48 us
    all_to_all x1, waiting for transfers between devices, to_others(): lax.all_to_all(pieces, 'rows', split_axis=0, concat_axis=0, tiled=True)  3.82 us
    pallas_call x1, Pallas kernels, local(): call(functools.partial(rows_kernel, height, width), [VMEM] * 4, jax.Shape...  3.41 us
    pallas_call x1, Pallas kernels, local(): call(functools.partial(outer_kernel, height, count, width), [SMEM] + [VME...  3.17 us
  transfers between devices with their start and end apart: 5, of which 3 were waited for; matrix products, arithmetic and copies ran while one was open for 0% of the time, Pallas kernels for 14%

profile of v2, /device:TPU:0, one launch (start us, length us, event | category | flops | bytes accessed | tf_op | source)
XLA Modules:
  0.0 80.5 jit_solution(4880128452095565627)
XLA Ops:
  0.0 0.0 copy-start.2
  0.0 0.0 copy-start.1
  0.0 0.0 copy-start
  0.0 3.1 %specimen_columns.1 = bf16[8,4,144,128]{3,2,1,0:T(8,128)(2,1)} custom-call(bf16[2,128,1024]{2,1,0:T(8,128)(2,1)} %index_ref.7, bf16[2,128,1024]{2,1,0:T(8,128)(2,1)} %loss_ref.7), custom_call_target="tpu_custom_call" | custom-call | tf_op jit(solution)/shard_map/specimen_columns/pallas_call | solution.py:600
  3.1 5.2 %all-to-all-start = ((bf16[8,4,144,128]{3,2,1,0:T(8,128)(2,1)}), bf16[8,4,144,128]{3,2,1,0:T(8,128)(2,1)S(1)}, u32[]{:S(2)}, u32[]{:S(2)}) async-start(bf16[8,4,144,128]{3,2,1,0:T(8,128)(2,1)} %specimen_columns.1), calls=%async_computation | async-start | bytes 2359296 | tf_op jit(solution)/shard_map/all_to_all | solution.py:567
  8.3 0.0 copy-done.2
  8.3 0.0 copy-done.1
  8.3 0.0 copy-done
  8.3 6.8 %slices_inner_rows.1 = bf16[240,1024]{1,0:T(8,128)(2,1)} custom-call(f32[2,128,1024]{2,1,0:T(8,128)S(1)} %bitcast.4, bf16[2,128,1024]{2,1,0:T(8,128)(2,1)S(1)} %copy-done.1, bf16[2,128,1024]{2,1,0:T(8,128)(2,1)S(1)} %copy-done.2), custom_call_target="tpu_custom_call" | custom-call | flops 41943040 | bytes 33554432 | tf_op jit(solution)/shard_map/slices_inner_rows/pallas_call | solution.py:613
  15.1 1.6 %collective-permute-start = (bf16[240,1024]{1,0:T(8,128)(2,1)}, bf16[240,1024]{1,0:T(8,128)(2,1)}, u32[]{:S(2)}, u32[]{:S(2)}) collective-permute-start(bf16[240,1024]{1,0:T(8,128)(2,1)} %slices_inner_rows.1), channel_id=1, source_target_pairs={{0,8},{8,16},{16,24},{24,0},{1,9},{9,17},{17,25},{25,1},{2,10},{10... | collective-permute-start | bytes 1474568 | tf_op jit(solution)/shard_map/ppermute | solution.py:622
  16.7 1.1 %edge_lines.1 = (f32[6,8,1024]{2,1,0:T(8,128)}, f32[6,8,1024]{2,1,0:T(8,128)}) custom-call(f32[2,128,1024]{2,1,0:T(8,128)S(1)} %bitcast.5, bf16[2,128,1024]{2,1,0:T(8,128)(2,1)S(1)} %copy-done.1, bf16[2,128,1024]{2,1,0:T(8,128)(2,1)S(1)} %copy-done.2), custom_call_target="tpu_custom_call" | custom-call | tf_op jit(solution)/shard_map/edge_lines/pallas_call | solution.py:625
  17.7 2.1 %collective-permute-start.1 = (f32[6,8,1024]{2,1,0:T(8,128)}, f32[6,8,1024]{2,1,0:T(8,128)S(1)}, u32[]{:S(2)}, u32[]{:S(2)}) collective-permute-start(f32[6,8,1024]{2,1,0:T(8,128)} %get-tuple-element.14), channel_id=1, source_target_pairs={{0,1},{1,2},{2,3},{3,4},{4,5},{5,6},{6,7},{8,9},{9,10},{10,11},{11... | collective-permute-start | bytes 589832 | tf_op jit(solution)/shard_map/ppermute | solution.py:642
  19.9 1.3 %collective-permute-start.2 = (f32[6,8,1024]{2,1,0:T(8,128)}, f32[6,8,1024]{2,1,0:T(8,128)}, u32[]{:S(2)}, u32[]{:S(2)}) collective-permute-start(f32[6,8,1024]{2,1,0:T(8,128)} %get-tuple-element.15), channel_id=1, source_target_pairs={{1,0},{2,1},{3,2},{4,3},{5,4},{6,5},{7,6},{9,8},{10,9},{11,10},{12... | collective-permute-start | bytes 589832 | tf_op jit(solution)/shard_map/ppermute | solution.py:643
  21.2 0.1 add_convert_fusion.edge_ref
  21.3 3.8 %all-to-all-done.specimen = bf16[8,4,144,128]{3,2,1,0:T(8,128)(2,1)S(1)} async-done(((bf16[8,4,144,128]{3,2,1,0:T(8,128)(2,1)}), bf16[8,4,144,128]{3,2,1,0:T(8,128)(2,1)S(1)}, u32[]{:S(2)}, u32[]{:S(2)}) %all-to-all-start) | async-done | bytes 1179680 | tf_op jit(solution)/shard_map/all_to_all | solution.py:567
  25.1 0.6 coefficients.1.ready
  25.7 0.0 copy-start.3
  25.7 0.0 copy-start.4
  25.7 0.0 collective-permute-done.1.above
  25.7 0.0 collective-permute-done.2.below
  25.7 3.2 %slices_outer_rows.1 = bf16[48,1024]{1,0:T(8,128)(2,1)S(1)} custom-call(s32[2]{0:T(128)S(1)} %add_convert_fusion.edge_ref, f32[2,128,1024]{2,1,0:T(8,128)S(1)} %bitcast.6, f32[6,8,1024]{2,1,0:T(8,128)S(1)} %collective-permute-done.1.above, f32[6,8,1024]{2,1,0:T(8,128)} %collective-permute-done.2.below, bf16[2,128,1024]{2,1,0:T(8,128)(2,1)S(1)} %copy-done.1, ...), custom_call_target="tpu_custom_call" | custom-call | flops 15728640 | bytes 12582912 | tf_op jit(solution)/shard_map/slices_outer_rows/pallas_call | solution.py:657
  28.9 1.6 %collective-permute-start.3 = (bf16[48,1024]{1,0:T(8,128)(2,1)S(1)}, bf16[48,1024]{1,0:T(8,128)(2,1)S(1)}, u32[]{:S(2)}, u32[]{:S(2)}) collective-permute-start(bf16[48,1024]{1,0:T(8,128)(2,1)S(1)} %slices_outer_rows.1), channel_id=1, source_target_pairs={{0,8},{8,16},{16,24},{24,0},{1,9},{9,17},{17,25},{25,1},{2,10},{10... | collective-permute-start | bytes 294920 | tf_op jit(solution)/shard_map/ppermute | solution.py:666
  30.5 0.4 collective-permute-done.inner_ref
  30.9 4.5 %collective-permute-done.3.outer_ref = bf16[48,1024]{1,0:T(8,128)(2,1)S(1)} collective-permute-done((bf16[48,1024]{1,0:T(8,128)(2,1)S(1)}, bf16[48,1024]{1,0:T(8,128)(2,1)S(1)}, u32[]{:S(2)}, u32[]{:S(2)}) %collective-permute-start.3) | collective-permute-done | bytes 98336 | tf_op jit(solution)/shard_map/ppermute | solution.py:666
  35.4 0.0 copy-done.3
  35.4 0.0 copy-done.4
  35.4 3.4 %gap_along_rows.1 = bf16[8,160,256]{2,1,0:T(8,128)(2,1)S(1)} custom-call(bf16[240,1024]{1,0:T(8,128)(2,1)} %collective-permute-done.inner_ref, bf16[48,1024]{1,0:T(8,128)(2,1)S(1)} %collective-permute-done.3.outer_ref, bf16[2,4,256,256]{3,2,1,0:T(8,128)(2,1)S(1)} %copy-done.4, bf16[2,2,512,512]{3,2,1,0:T(8,128)(2,1)S(1)} %copy-done.3), custom_call_target="tpu_custom_call" | custom-call | flops 1610612736 | bytes 8388608 | tf_op jit(solution)/shard_map/gap_along_rows/pallas_call | solution.py:668
  38.8 17.0 %all_to_all.15.blocks = bf16[8,160,256]{2,1,0:T(8,128)(2,1)S(1)} all-to-all(bf16[8,160,256]{2,1,0:T(8,128)(2,1)S(1)} %gap_along_rows.1), channel_id=1, replica_groups=mesh['depth'=4,'rows'=8] {'rows'}, dimensions={0} | all-to-all | bytes 1310720 | tf_op jit(solution)/shard_map/all_to_all | solution.py:567
  55.7 0.0 copy-start.5
  55.7 0.0 copy-start.6
  55.7 9.1 %gap_slices_gap_columns.1 = bf16[8,144,256]{2,1,0:T(8,128)(2,1)S(1)} custom-call(s32[2]{0:T(128)S(1)} %add_convert_fusion.edge_ref, bf16[8,160,256]{2,1,0:T(8,128)(2,1)S(1)} %all_to_all.15.blocks, f32[2,2,8,144,128]{4,3,2,1,0:T(8,128)S(1)} %coefficients.1.ready, bf16[2,4,256,256]{3,2,1,0:T(8,128)(2,1)S(1)} %copy-done.4, bf16[2,2,512,512]{3,2,1,0:T(8,128)(2,1)S(1)} %copy-done.3), custom_call_target="tpu_custom_call" | custom-call | flops 47185920 | bytes 37748736 | tf_op jit(solution)/shard_map/gap_slices_gap_columns/pallas_call | solution.py:682
  64.9 12.8 %all_to_all.16.blocks = bf16[8,144,256]{2,1,0:T(8,128)(2,1)S(1)} all-to-all(bf16[8,144,256]{2,1,0:T(8,128)(2,1)S(1)} %gap_slices_gap_columns.1), channel_id=1, replica_groups=mesh['depth'=4,'rows'=8] {'rows'}, dimensions={0} | all-to-all | bytes 1179648 | tf_op jit(solution)/shard_map/all_to_all | solution.py:567
  77.7 0.0 copy-done.5
  77.7 0.0 copy-done.6
  77.7 2.8 %gap_rows.1 = f32[2,128,1024]{2,1,0:T(8,128)} custom-call(bf16[8,144,256]{2,1,0:T(8,128)(2,1)S(1)} %all_to_all.16.blocks, bf16[2,4,256,256]{3,2,1,0:T(8,128)(2,1)S(1)} %copy-done.6, bf16[2,2,512,512]{3,2,1,0:T(8,128)(2,1)S(1)} %copy-done.5), custom_call_target="tpu_custom_call" | custom-call | flops 1610612736 | bytes 6291456 | tf_op jit(solution)/shard_map/gap_rows/pallas_call | solution.py:693
Async XLA Ops:
  0.0 8.3 %copy-start.2 = (bf16[2,128,1024]{2,1,0:T(8,128)(2,1)S(1)}, bf16[2,128,1024]{2,1,0:T(8,128)(2,1)}, u32[]{:S(2)}) copy-start(bf16[2,128,1024]{2,1,0:T(8,128)(2,1)} %loss_ref.7) | copy-start | bytes 1572868
  0.0 8.3 %copy-start.1 = (bf16[2,128,1024]{2,1,0:T(8,128)(2,1)S(1)}, bf16[2,128,1024]{2,1,0:T(8,128)(2,1)}, u32[]{:S(2)}) copy-start(bf16[2,128,1024]{2,1,0:T(8,128)(2,1)} %index_ref.7) | copy-start | bytes 1572868
  0.0 8.3 %copy-start = (f32[1,2,128,1024]{3,2,1,0:T(8,128)S(1)}, f32[1,2,128,1024]{3,2,1,0:T(8,128)}, u32[]{:S(2)}) copy-start(f32[1,2,128,1024]{3,2,1,0:T(8,128)} %param.7) | copy-start | bytes 3145732
  3.1 22.0 %all-to-all-start = ((bf16[8,4,144,128]{3,2,1,0:T(8,128)(2,1)}), bf16[8,4,144,128]{3,2,1,0:T(8,128)(2,1)S(1)}, u32[]{:S(2)}, u32[]{:S(2)}) async-start(bf16[8,4,144,128]{3,2,1,0:T(8,128)(2,1)} %specimen_columns.1), calls=%async_computation | async-start | bytes 2359296 | tf_op jit(solution)/shard_map/all_to_all | solution.py:567
  15.1 15.8 %collective-permute-start = (bf16[240,1024]{1,0:T(8,128)(2,1)}, bf16[240,1024]{1,0:T(8,128)(2,1)}, u32[]{:S(2)}, u32[]{:S(2)}) collective-permute-start(bf16[240,1024]{1,0:T(8,128)(2,1)} %slices_inner_rows.1), channel_id=1, source_target_pairs={{0,8},{8,16},{16,24},{24,0},{1,9},{9,17},{17,25},{25,1},{2,10},{10... | collective-permute-start | bytes 1474568 | tf_op jit(solution)/shard_map/ppermute | solution.py:622
  17.7 8.0 %collective-permute-start.1 = (f32[6,8,1024]{2,1,0:T(8,128)}, f32[6,8,1024]{2,1,0:T(8,128)S(1)}, u32[]{:S(2)}, u32[]{:S(2)}) collective-permute-start(f32[6,8,1024]{2,1,0:T(8,128)} %get-tuple-element.14), channel_id=1, source_target_pairs={{0,1},{1,2},{2,3},{3,4},{4,5},{5,6},{6,7},{8,9},{9,10},{10,11},{11... | collective-permute-start | bytes 589832 | tf_op jit(solution)/shard_map/ppermute | solution.py:642
  19.9 5.8 %collective-permute-start.2 = (f32[6,8,1024]{2,1,0:T(8,128)}, f32[6,8,1024]{2,1,0:T(8,128)}, u32[]{:S(2)}, u32[]{:S(2)}) collective-permute-start(f32[6,8,1024]{2,1,0:T(8,128)} %get-tuple-element.15), channel_id=1, source_target_pairs={{1,0},{2,1},{3,2},{4,3},{5,4},{6,5},{7,6},{9,8},{10,9},{11,10},{12... | collective-permute-start | bytes 589832 | tf_op jit(solution)/shard_map/ppermute | solution.py:643
  25.7 9.7 %copy-start.3 = (bf16[2,2,512,512]{3,2,1,0:T(8,128)(2,1)S(1)}, bf16[2,2,512,512]{3,2,1,0:T(8,128)(2,1)}, u32[]{:S(2)}) copy-start(bf16[2,2,512,512]{3,2,1,0:T(8,128)(2,1)} %constant.19.clone.large) | copy-start | bytes 6291460
  25.7 9.7 %copy-start.4 = (bf16[2,4,256,256]{3,2,1,0:T(8,128)(2,1)S(1)}, bf16[2,4,256,256]{3,2,1,0:T(8,128)(2,1)}, u32[]{:S(2)}) copy-start(bf16[2,4,256,256]{3,2,1,0:T(8,128)(2,1)} %constant.18.clone.small) | copy-start | bytes 3145732
  28.9 6.5 %collective-permute-start.3 = (bf16[48,1024]{1,0:T(8,128)(2,1)S(1)}, bf16[48,1024]{1,0:T(8,128)(2,1)S(1)}, u32[]{:S(2)}, u32[]{:S(2)}) collective-permute-start(bf16[48,1024]{1,0:T(8,128)(2,1)S(1)} %slices_outer_rows.1), channel_id=1, source_target_pairs={{0,8},{8,16},{16,24},{24,0},{1,9},{9,17},{17,25},{25,1},{2,10},{10... | collective-permute-start | bytes 294920 | tf_op jit(solution)/shard_map/ppermute | solution.py:666
  55.7 22.0 %copy-start.5 = (bf16[2,2,512,512]{3,2,1,0:T(8,128)(2,1)S(1)}, bf16[2,2,512,512]{3,2,1,0:T(8,128)(2,1)}, u32[]{:S(2)}) copy-start(bf16[2,2,512,512]{3,2,1,0:T(8,128)(2,1)} %constant.17.clone.large) | copy-start | bytes 6291460
  55.7 22.0 %copy-start.6 = (bf16[2,4,256,256]{3,2,1,0:T(8,128)(2,1)S(1)}, bf16[2,4,256,256]{3,2,1,0:T(8,128)(2,1)}, u32[]{:S(2)}) copy-start(bf16[2,4,256,256]{3,2,1,0:T(8,128)(2,1)} %constant.16.clone.small) | copy-start | bytes 3145732

commit v3 on v2

--- a/solution.py
+++ b/solution.py
@@ -232,15 +232,12 @@
             body(k)
         wrap(target, steps)
 
-    def one_slice(slice_index, carry):
+    for slice_index in range(count):
         source = bufs[0]
         for degree in range(TAYLOR, 0, -1):
             target = bufs[0] if degree == 1 else bufs[1 + degree % 2]
             step(slice_index, source, target, LATERAL / degree)
             source = target
-        return carry
-
-    lax.fori_loop(0, count, one_slice, 0)
 
 
 def scaled_phase(values):
@@ -273,7 +270,7 @@
         parts = [specimen[:, first : first + side]]
         if rows:
             rest = field[:, first : first + side]
-            for _ in range(3):
+            for _ in range(2):
                 part = rest.astype(BF16)
                 parts.append(part)
                 rest = rest - part.astype(F32)
@@ -286,8 +283,8 @@
         own = specimen.shape[0]
         cells = None
         if rows:
-            high, mid, low = (lines[own + i * rows : own + (i + 1) * rows] for i in range(3))
-            cells = high + (mid + low)
+            high, low = (lines[own + i * rows : own + (i + 1) * rows] for i in range(2))
+            cells = high + low
         yield first // LANES, cells, lines[:own]
 
 
@@ -320,54 +317,59 @@
     )
 
 
-def lines_kernel(
-    height, count, width, field, index_ref, loss_ref, head, tail, cells, deltas, absorbs, sems
+def turn_kernel(
+    height, count, width, field, index_ref, loss_ref, out, head, tail,
+    source, turned, staged, ends, came, sent, ends_came, ends_sent,
 ):
-    copies = []
-    for end, start in enumerate((0, height - width)):
-        copies.append((field.at[:, pl.ds(start, width)], cells.at[end]))
-    for end, start in enumerate((0, height - 16)):
-        copies.append((index_ref.at[:, pl.ds(start, 16)], deltas.at[end]))
-        copies.append((loss_ref.at[:, pl.ds(start, 16)], absorbs.at[end]))
-    started = [
-        pltpu.make_async_copy(source, target, sems.at[i])
-        for i, (source, target) in enumerate(copies)
+    length = index_ref.shape[2]
+    half = height // 2
+    side = 2 * LANES
+    lines = [(ref, k) for ref in (index_ref, loss_ref) for k in range(count)]
+    arrivals = []
+    for line, (ref, k) in enumerate(lines):
+        for part in range(2):
+            rows = pl.ds(part * half, half)
+            arrivals.append(
+                pltpu.make_async_copy(
+                    ref.at[k, rows], source.at[line, rows], came.at[2 * line + part]
+                )
+            )
+    for copy in arrivals:
+        copy.start()
+    end_arrivals = [
+        pltpu.make_async_copy(
+            field.at[:, pl.ds(end * (height - width), width)],
+            ends.at[end, pl.ds(0, 2)],
+            ends_came.at[end],
+        )
+        for end in range(2)
     ]
-    for copy in started:
+    for copy in end_arrivals:
         copy.start()
-    for copy in started:
+    margin = jnp.zeros((width, height), F32)
+    departures = []
+    for line in range(len(lines)):
+        for copy in arrivals[2 * line : 2 * line + 2]:
+            copy.wait()
+        ends[0, 2 + line] = source[line, 0:16, :].astype(F32)[:width]
+        ends[1, 2 + line] = source[line, height - 16 :, :].astype(F32)[16 - width :]
+        turned[line, 0:width, :] = margin
+        turned[line, width + length :, :] = margin
+        for start in range(0, length, side):
+            turned[line, width + start : width + start + side, :] = (
+                source[line, :, start : start + side].astype(F32).T
+            )
+        for k in range(out.shape[0]):
+            window = turned[line, k * height : k * height + height + 2 * width, :]
+            staged[line, k] = window.astype(BF16)
+        departures.append(pltpu.make_async_copy(staged.at[line], out.at[:, line], sent.at[line]))
+        departures[-1].start()
+    for end, target in enumerate((head, tail)):
+        end_arrivals[end].wait()
+        departures.append(pltpu.make_async_copy(ends.at[end], target, ends_sent.at[end]))
+        departures[-1].start()
+    for copy in departures:
         copy.wait()
-    for end, out in enumerate((head, tail)):
-        out[0:2] = cells[end]
-        skip = 0 if end == 0 else 16 - width
-        for k in range(count):
-            out[2 + k] = deltas[end, k].astype(F32)[skip : skip + width]
-            out[2 + count + k] = absorbs[end, k].astype(F32)[skip : skip + width]
-
-
-def turn_kernel(height, count, width, index_ref, loss_ref, out, turned):
-    length = index_ref.shape[2]
-    side = 2 * LANES
-    diagonal = lax.broadcasted_iota(jnp.int32, (side, side), 0) == lax.broadcasted_iota(
-        jnp.int32, (side, side), 1
-    )
-    identity = jnp.where(diagonal, 1.0, 0.0).astype(BF16)
-    margin = jnp.zeros((width, height), F32)
-    for which, source in enumerate((index_ref, loss_ref)):
-        for k in range(count):
-            line = which * count + k
-            turned[line, 0:width, :] = margin
-            turned[line, width + length :, :] = margin
-            for start in range(0, length, side):
-                turned[line, width + start : width + start + side, :] = lax.dot_general(
-                    identity,
-                    source[k, :, start : start + side],
-                    (((1,), (1,)), ((), ())),
-                    preferred_element_type=F32,
-                )
-    for k in range(out.shape[0]):
-        for line in range(2 * count):
-            out[k, line] = turned[line, k * height : k * height + height + 2 * width, :].astype(BF16)
 
 
 def put_coded(out, first, natural, rows, scale):
@@ -385,7 +387,7 @@
 
 
 def inner_kernel(
-    height, count, width, field, index_ref, loss_ref, out,
+    height, count, width, field, index_ref, loss_ref, out, scale_out,
     buf0, buf1, buf2, phase, loss, keep, natural,
 ):
     bufs = (buf0, buf1, buf2)
@@ -404,11 +406,11 @@
     scale = scale_of([natural[part, :, width : height - width, :] for part in range(2)])
     for part in range(2):
         put_coded(out, part * inner, natural.at[part], rows, scale)
-    put_scale(out, 2 * inner, scale)
+    scale_out[...] = jnp.broadcast_to(scale, scale_out.shape)
 
 
 def outer_kernel(
-    height, count, width, edge_ref, field, above, below, index_ref, loss_ref, ready, out,
+    height, count, width, edge_ref, field, above, below, index_ref, loss_ref, inner_scale, ready, out,
     buf0, buf1, buf2, phase, loss, keep, natural,
 ):
     del ready
@@ -440,6 +442,7 @@
             both = jnp.concatenate([natural[part, i, s:e, :] for s, e in ends], axis=0)
             out[part * own : (part + 1) * own, i * LANES : (i + 1) * LANES] = encode(both, scale)
     put_scale(out, 2 * own, scale)
+    put_scale(out, 2 * own + SCALE_ROWS, inner_scale[0:1, 0:1])
 
 
 def rows_kernel(
@@ -452,8 +455,8 @@
     def scale_in(ref, row):
         return ref[row : row + SCALE_ROWS, :].astype(F32)[0:1]
 
-    inner_scale = scale_in(inner_ref, 2 * inner)
     outer_scale = scale_in(outer_ref, 4 * width)
+    inner_scale = scale_in(outer_ref, 4 * width + SCALE_ROWS)
     for part in range(2):
         start = part * height
         ends = decode(outer_ref[2 * part * width : 2 * (part + 1) * width, :], outer_scale)
@@ -540,11 +543,11 @@
 ANY = pl.BlockSpec(memory_space=pl.ANY)
 
 
-def call(kernel, in_specs, out_shape, scratch, name, flops, moved, outs=1, room=VMEM_BYTES):
+def call(kernel, in_specs, out_shape, scratch, name, flops, moved, outs=None, room=VMEM_BYTES):
     return pl.pallas_call(
         kernel,
         in_specs=in_specs,
-        out_specs=VMEM if outs == 1 else (VMEM,) * outs,
+        out_specs=outs or VMEM,
         out_shape=out_shape,
         scratch_shapes=scratch,
         compiler_params=pltpu.CompilerParams(vmem_limit_bytes=room),
@@ -597,46 +600,48 @@
     gap_flops = 24 * height * length * length // 2
     to_next = [(g, (g + 1) % groups) for g in range(groups)]
 
-    turned = call(
+    line_shape = jax.ShapeDtypeStruct((2 + 2 * count, width, length), F32)
+    turned, head, tail = call(
         functools.partial(turn_kernel, height, count, width),
-        [VMEM] * 2,
-        jax.ShapeDtypeStruct((slabs, 2 * count, tall, height), BF16),
-        [pltpu.VMEM((2 * count, length + 2 * width, height), F32)],
+        [ANY] * 3,
+        (
+            jax.ShapeDtypeStruct((slabs, 2 * count, tall, height), BF16),
+            line_shape,
+            line_shape,
+        ),
+        [
+            pltpu.VMEM((2 * count, height, length), BF16),
+            pltpu.VMEM((2 * count, length + 2 * width, height), F32),
+            pltpu.VMEM((2 * count, slabs, tall, height), BF16),
+            pltpu.VMEM((2, 2 + 2 * count, width, length), F32),
+            pltpu.SemaphoreType.DMA((4 * count,)),
+            pltpu.SemaphoreType.DMA((2 * count,)),
+            pltpu.SemaphoreType.DMA((2,)),
+            pltpu.SemaphoreType.DMA((2,)),
+        ],
         "specimen_columns",
         0,
         0,
+        outs=(ANY, ANY, ANY),
         room=ALL_VMEM_BYTES,
-    )(phase_index, absorption)
+    )(field, phase_index, absorption)
     turned, field = lax.optimization_barrier((turned, field))
     specimen = to_others(turned)
 
-    inner = call(
+    inner, inner_scale = call(
         functools.partial(inner_kernel, height, count, width),
         [VMEM] * 3,
-        jax.ShapeDtypeStruct((2 * (height - 2 * width) + SCALE_ROWS, length), BF16),
+        (
+            jax.ShapeDtypeStruct((2 * (height - 2 * width), length), BF16),
+            jax.ShapeDtypeStruct((8, LANES), F32),
+        ),
         working(height, True),
         "slices_inner_rows",
         *slice_cost(height),
+        (VMEM, VMEM),
     )(field, phase_index, absorption)
-    inner, late_field = lax.optimization_barrier((inner, field))
+    inner, head, tail = lax.optimization_barrier((inner, head, tail))
     inner = lax.ppermute(inner, "depth", to_next)
-
-    line_shape = jax.ShapeDtypeStruct((2 + 2 * count, width, length), F32)
-    head, tail = call(
-        functools.partial(lines_kernel, height, count, width),
-        [ANY] * 3,
-        (line_shape, line_shape),
-        [
-            pltpu.VMEM((2, 2, width, length), F32),
-            pltpu.VMEM((2, count, 16, length), BF16),
-            pltpu.VMEM((2, count, 16, length), BF16),
-            pltpu.SemaphoreType.DMA((6,)),
-        ],
-        "edge_lines",
-        0,
-        0,
-        2,
-    )(late_field, phase_index, absorption)
     down = [(i, i + 1) for i in range(slabs - 1)]
     up = [(i + 1, i) for i in range(slabs - 1)]
     above = lax.ppermute(tail, "rows", down)
@@ -656,12 +661,12 @@
 
     outer = call(
         functools.partial(outer_kernel, height, count, width),
-        [SMEM] + [VMEM] * 5 + [ANY],
-        jax.ShapeDtypeStruct((4 * width + SCALE_ROWS, length), BF16),
+        [SMEM] + [VMEM] * 6 + [ANY],
+        jax.ShapeDtypeStruct((4 * width + 2 * SCALE_ROWS, length), BF16),
         working(6 * width, True),
         "slices_outer_rows",
         *slice_cost(6 * width),
-    )(edge, late_field, above, below, phase_index, absorption, coefficients)
+    )(edge, field, above, below, phase_index, absorption, inner_scale, coefficients)
 
     outer = lax.ppermute(outer, "depth", to_next)
 

time: 80.8 us -> 79.9 us (0.989)
  Pallas kernels: 30 us -> 27.9 us
  waiting for transfers between devices: 8.66 us -> 10.6 us
    pallas_call x3 -> x2, Pallas kernels: 11 us -> 8.99 us  [the longest x1 6.31 us: local(): call(functools.partial(inner_kernel, height, count, width), [VMEM] * 3, (...]
    all_to_all x1, waiting for transfers between devices: 3.82 us -> 5.39 us  [to_others(): lax.all_to_all(pieces, 'rows', split_axis=0, concat_axis=0, tiled=True)]
  transfers between devices with their start and end apart: 5 -> 5, of which waited for: 3 -> 2; matrix products, arithmetic and copies ran while one was open for 0% -> 0% of each run, Pallas kernels for 14% -> 13%
where the time goes in v3:
time: 79.9 us; the launch traced here: 79.5 us
  blocking collectives  29.1 us (36%)
  Pallas kernels  27.9 us (35%)
  starting transfers between devices  11.8 us (15%)
  waiting for transfers between devices  10.6 us (13%)
    all_to_all x2, blocking collectives, to_others(): lax.all_to_all(pieces, 'rows', split_axis=0, concat_axis=0, tiled=True)  29.1 us
    pallas_call x1, Pallas kernels, local(): call(functools.partial(second_kernel, height, count, width), [SMEM] + [VM...  9 us
    pallas_call x1, Pallas kernels, local(): call(functools.partial(inner_kernel, height, count, width), [VMEM] * 3, (...  6.31 us
    all_to_all x1, waiting for transfers between devices, to_others(): lax.all_to_all(pieces, 'rows', split_axis=0, concat_axis=0, tiled=True)  5.39 us
    all_to_all x1, starting transfers between devices, to_others(): lax.all_to_all(pieces, 'rows', split_axis=0, concat_axis=0, tiled=True)  5.19 us
    ppermute x1, waiting for transfers between devices, local(): outer = lax.ppermute(outer, 'depth', to_next)  5.19 us
    pallas_call x1, Pallas kernels, local(): call(functools.partial(rows_kernel, height, width), [VMEM] * 4, jax.Shape...  3.39 us
    pallas_call x1, Pallas kernels, local(): call(functools.partial(outer_kernel, height, count, width), [SMEM] + [VME...  3.11 us
  transfers between devices with their start and end apart: 5, of which 2 were waited for; matrix products, arithmetic and copies ran while one was open for 0% of the time, Pallas kernels for 13%

profile of v3, /device:TPU:0, one launch (start us, length us, event | category | flops | bytes accessed | tf_op | source)
XLA Modules:
  0.0 79.5 jit_solution(17961377298510913539)
XLA Ops:
  0.0 0.0 copy-start
  0.0 0.0 copy-start.1
  0.0 0.0 copy-start.2
  0.0 2.7 %specimen_columns.1 = (bf16[8,4,144,128]{3,2,1,0:T(8,128)(2,1)}, f32[6,8,1024]{2,1,0:T(8,128)}, f32[6,8,1024]{2,1,0:T(8,128)}) custom-call(f32[2,128,1024]{2,1,0:T(8,128)} %bitcast.4, bf16[2,128,1024]{2,1,0:T(8,128)(2,1)} %index_ref.5, bf16[2,128,1024]{2,1,0:T(8,128)(2,1)} %loss_ref.5), custom_call_target="tpu_custom_call" | custom-call | tf_op jit(solution)/shard_map/specimen_columns/pallas_call | solution.py:604
  2.7 5.2 %all-to-all-start = ((bf16[8,4,144,128]{3,2,1,0:T(8,128)(2,1)}), bf16[8,4,144,128]{3,2,1,0:T(8,128)(2,1)S(1)}, u32[]{:S(2)}, u32[]{:S(2)}) async-start(bf16[8,4,144,128]{3,2,1,0:T(8,128)(2,1)} %get-tuple-element.24), calls=%async_computation | async-start | bytes 2359296 | tf_op jit(solution)/shard_map/all_to_all | solution.py:570
  7.9 0.0 copy-done
  7.9 0.0 copy-done.1
  7.9 0.0 copy-done.2
  7.9 6.3 %slices_inner_rows.1 = (bf16[224,1024]{1,0:T(8,128)(2,1)}, f32[8,128]{1,0:T(8,128)S(1)}) custom-call(f32[2,128,1024]{2,1,0:T(8,128)S(1)} %bitcast.5, bf16[2,128,1024]{2,1,0:T(8,128)(2,1)S(1)} %copy-done.1, bf16[2,128,1024]{2,1,0:T(8,128)(2,1)S(1)} %copy-done.2), custom_call_target="tpu_custom_call" | custom-call | flops 41943040 | bytes 33554432 | tf_op jit(solution)/shard_map/slices_inner_rows/pallas_call | solution.py:631
  14.2 1.6 %collective-permute-start = (bf16[224,1024]{1,0:T(8,128)(2,1)}, bf16[224,1024]{1,0:T(8,128)(2,1)}, u32[]{:S(2)}, u32[]{:S(2)}) collective-permute-start(bf16[224,1024]{1,0:T(8,128)(2,1)} %get-tuple-element.20), channel_id=1, source_target_pairs={{0,8},{8,16},{16,24},{24,0},{1,9},{9,17},{17,25},{25,1},{2,10},{10... | collective-permute-start | bytes 1376264 | tf_op jit(solution)/shard_map/ppermute | solution.py:644
  15.8 2.1 %collective-permute-start.1 = (f32[6,8,1024]{2,1,0:T(8,128)}, f32[6,8,1024]{2,1,0:T(8,128)S(1)}, u32[]{:S(2)}, u32[]{:S(2)}) collective-permute-start(f32[6,8,1024]{2,1,0:T(8,128)} %get-tuple-element.21), channel_id=1, source_target_pairs={{0,1},{1,2},{2,3},{3,4},{4,5},{5,6},{6,7},{8,9},{9,10},{10,11},{11... | collective-permute-start | bytes 589832 | tf_op jit(solution)/shard_map/ppermute | solution.py:647
  17.9 1.3 %collective-permute-start.2 = (f32[6,8,1024]{2,1,0:T(8,128)}, f32[6,8,1024]{2,1,0:T(8,128)}, u32[]{:S(2)}, u32[]{:S(2)}) collective-permute-start(f32[6,8,1024]{2,1,0:T(8,128)} %get-tuple-element.22), channel_id=1, source_target_pairs={{1,0},{2,1},{3,2},{4,3},{5,4},{6,5},{7,6},{9,8},{10,9},{11,10},{12... | collective-permute-start | bytes 589832 | tf_op jit(solution)/shard_map/ppermute | solution.py:648
  19.2 0.1 add_convert_fusion.edge_ref
  19.3 5.4 %all-to-all-done.specimen = bf16[8,4,144,128]{3,2,1,0:T(8,128)(2,1)S(1)} async-done(((bf16[8,4,144,128]{3,2,1,0:T(8,128)(2,1)}), bf16[8,4,144,128]{3,2,1,0:T(8,128)(2,1)S(1)}, u32[]{:S(2)}, u32[]{:S(2)}) %all-to-all-start) | async-done | bytes 1179680 | tf_op jit(solution)/shard_map/all_to_all | solution.py:570
  24.7 0.6 coefficients.1.ready
  25.3 0.0 collective-permute-done.1.above
  25.3 0.0 collective-permute-done.2.below
  25.3 0.0 copy-start.3
  25.3 0.0 copy-start.4
  25.3 3.1 %slices_outer_rows.1 = bf16[64,1024]{1,0:T(8,128)(2,1)S(1)} custom-call(s32[2]{0:T(128)S(1)} %add_convert_fusion.edge_ref, f32[2,128,1024]{2,1,0:T(8,128)S(1)} %bitcast.6, f32[6,8,1024]{2,1,0:T(8,128)S(1)} %collective-permute-done.1.above, f32[6,8,1024]{2,1,0:T(8,128)} %collective-permute-done.2.below, bf16[2,128,1024]{2,1,0:T(8,128)(2,1)S(1)} %copy-done.1, ...), custom_call_target="tpu_custom_call" | custom-call | flops 15728640 | bytes 12582912 | tf_op jit(solution)/shard_map/slices_outer_rows/pallas_call | solution.py:662
  28.5 1.6 %collective-permute-start.3 = (bf16[64,1024]{1,0:T(8,128)(2,1)S(1)}, bf16[64,1024]{1,0:T(8,128)(2,1)S(1)}, u32[]{:S(2)}, u32[]{:S(2)}) collective-permute-start(bf16[64,1024]{1,0:T(8,128)(2,1)S(1)} %slices_outer_rows.1), channel_id=1, source_target_pairs={{0,8},{8,16},{16,24},{24,0},{1,9},{9,17},{17,25},{25,1},{2,10},{10... | collective-permute-start | bytes 393224 | tf_op jit(solution)/shard_map/ppermute | solution.py:671
  30.1 0.0 collective-permute-done.inner_ref
  30.1 5.2 %collective-permute-done.3.outer_ref = bf16[64,1024]{1,0:T(8,128)(2,1)S(1)} collective-permute-done((bf16[64,1024]{1,0:T(8,128)(2,1)S(1)}, bf16[64,1024]{1,0:T(8,128)(2,1)S(1)}, u32[]{:S(2)}, u32[]{:S(2)}) %collective-permute-start.3) | collective-permute-done | bytes 131104 | tf_op jit(solution)/shard_map/ppermute | solution.py:671
  35.3 0.0 copy-done.3
  35.3 0.0 copy-done.4
  35.3 3.4 %gap_along_rows.1 = bf16[8,160,256]{2,1,0:T(8,128)(2,1)S(1)} custom-call(bf16[224,1024]{1,0:T(8,128)(2,1)} %collective-permute-done.inner_ref, bf16[64,1024]{1,0:T(8,128)(2,1)S(1)} %collective-permute-done.3.outer_ref, bf16[2,4,256,256]{3,2,1,0:T(8,128)(2,1)S(1)} %copy-done.4, bf16[2,2,512,512]{3,2,1,0:T(8,128)(2,1)S(1)} %copy-done.3), custom_call_target="tpu_custom_call" | custom-call | flops 1610612736 | bytes 8388608 | tf_op jit(solution)/shard_map/gap_along_rows/pallas_call | solution.py:673
  38.7 16.2 %all_to_all.15.blocks = bf16[8,160,256]{2,1,0:T(8,128)(2,1)S(1)} all-to-all(bf16[8,160,256]{2,1,0:T(8,128)(2,1)S(1)} %gap_along_rows.1), channel_id=1, replica_groups=mesh['depth'=4,'rows'=8] {'rows'}, dimensions={0} | all-to-all | bytes 1310720 | tf_op jit(solution)/shard_map/all_to_all | solution.py:570
  54.9 0.0 copy-start.5
  54.9 0.0 copy-start.6
  54.9 9.0 %gap_slices_gap_columns.1 = bf16[8,144,256]{2,1,0:T(8,128)(2,1)S(1)} custom-call(s32[2]{0:T(128)S(1)} %add_convert_fusion.edge_ref, bf16[8,160,256]{2,1,0:T(8,128)(2,1)S(1)} %all_to_all.15.blocks, f32[2,2,8,144,128]{4,3,2,1,0:T(8,128)S(1)} %coefficients.1.ready, bf16[2,4,256,256]{3,2,1,0:T(8,128)(2,1)S(1)} %copy-done.4, bf16[2,2,512,512]{3,2,1,0:T(8,128)(2,1)S(1)} %copy-done.3), custom_call_target="tpu_custom_call" | custom-call | flops 47185920 | bytes 37748736 | tf_op jit(solution)/shard_map/gap_slices_gap_columns/pallas_call | solution.py:687
  63.9 12.8 %all_to_all.16.blocks = bf16[8,144,256]{2,1,0:T(8,128)(2,1)S(1)} all-to-all(bf16[8,144,256]{2,1,0:T(8,128)(2,1)S(1)} %gap_slices_gap_columns.1), channel_id=1, replica_groups=mesh['depth'=4,'rows'=8] {'rows'}, dimensions={0} | all-to-all | bytes 1179648 | tf_op jit(solution)/shard_map/all_to_all | solution.py:570
  76.7 0.0 copy-done.5
  76.7 0.0 copy-done.6
  76.7 2.8 %gap_rows.1 = f32[2,128,1024]{2,1,0:T(8,128)} custom-call(bf16[8,144,256]{2,1,0:T(8,128)(2,1)S(1)} %all_to_all.16.blocks, bf16[2,4,256,256]{3,2,1,0:T(8,128)(2,1)S(1)} %copy-done.6, bf16[2,2,512,512]{3,2,1,0:T(8,128)(2,1)S(1)} %copy-done.5), custom_call_target="tpu_custom_call" | custom-call | flops 1610612736 | bytes 6291456 | tf_op jit(solution)/shard_map/gap_rows/pallas_call | solution.py:698
Async XLA Ops:
  0.0 7.9 %copy-start = (f32[1,2,128,1024]{3,2,1,0:T(8,128)S(1)}, f32[1,2,128,1024]{3,2,1,0:T(8,128)}, u32[]{:S(2)}) copy-start(f32[1,2,128,1024]{3,2,1,0:T(8,128)} %param.7) | copy-start | bytes 3145732
  0.0 7.9 %copy-start.1 = (bf16[2,128,1024]{2,1,0:T(8,128)(2,1)S(1)}, bf16[2,128,1024]{2,1,0:T(8,128)(2,1)}, u32[]{:S(2)}) copy-start(bf16[2,128,1024]{2,1,0:T(8,128)(2,1)} %index_ref.5) | copy-start | bytes 1572868
  0.0 7.9 %copy-start.2 = (bf16[2,128,1024]{2,1,0:T(8,128)(2,1)S(1)}, bf16[2,128,1024]{2,1,0:T(8,128)(2,1)}, u32[]{:S(2)}) copy-start(bf16[2,128,1024]{2,1,0:T(8,128)(2,1)} %loss_ref.5) | copy-start | bytes 1572868
  2.7 22.0 %all-to-all-start = ((bf16[8,4,144,128]{3,2,1,0:T(8,128)(2,1)}), bf16[8,4,144,128]{3,2,1,0:T(8,128)(2,1)S(1)}, u32[]{:S(2)}, u32[]{:S(2)}) async-start(bf16[8,4,144,128]{3,2,1,0:T(8,128)(2,1)} %get-tuple-element.24), calls=%async_computation | async-start | bytes 2359296 | tf_op jit(solution)/shard_map/all_to_all | solution.py:570
  14.2 15.9 %collective-permute-start = (bf16[224,1024]{1,0:T(8,128)(2,1)}, bf16[224,1024]{1,0:T(8,128)(2,1)}, u32[]{:S(2)}, u32[]{:S(2)}) collective-permute-start(bf16[224,1024]{1,0:T(8,128)(2,1)} %get-tuple-element.20), channel_id=1, source_target_pairs={{0,8},{8,16},{16,24},{24,0},{1,9},{9,17},{17,25},{25,1},{2,10},{10... | collective-permute-start | bytes 1376264 | tf_op jit(solution)/shard_map/ppermute | solution.py:644
  15.8 9.5 %collective-permute-start.1 = (f32[6,8,1024]{2,1,0:T(8,128)}, f32[6,8,1024]{2,1,0:T(8,128)S(1)}, u32[]{:S(2)}, u32[]{:S(2)}) collective-permute-start(f32[6,8,1024]{2,1,0:T(8,128)} %get-tuple-element.21), channel_id=1, source_target_pairs={{0,1},{1,2},{2,3},{3,4},{4,5},{5,6},{6,7},{8,9},{9,10},{10,11},{11... | collective-permute-start | bytes 589832 | tf_op jit(solution)/shard_map/ppermute | solution.py:647
  17.9 7.4 %collective-permute-start.2 = (f32[6,8,1024]{2,1,0:T(8,128)}, f32[6,8,1024]{2,1,0:T(8,128)}, u32[]{:S(2)}, u32[]{:S(2)}) collective-permute-start(f32[6,8,1024]{2,1,0:T(8,128)} %get-tuple-element.22), channel_id=1, source_target_pairs={{1,0},{2,1},{3,2},{4,3},{5,4},{6,5},{7,6},{9,8},{10,9},{11,10},{12... | collective-permute-start | bytes 589832 | tf_op jit(solution)/shard_map/ppermute | solution.py:648
  25.3 10.0 %copy-start.3 = (bf16[2,2,512,512]{3,2,1,0:T(8,128)(2,1)S(1)}, bf16[2,2,512,512]{3,2,1,0:T(8,128)(2,1)}, u32[]{:S(2)}) copy-start(bf16[2,2,512,512]{3,2,1,0:T(8,128)(2,1)} %constant.19.clone.large) | copy-start | bytes 6291460
  25.3 9.9 %copy-start.4 = (bf16[2,4,256,256]{3,2,1,0:T(8,128)(2,1)S(1)}, bf16[2,4,256,256]{3,2,1,0:T(8,128)(2,1)}, u32[]{:S(2)}) copy-start(bf16[2,4,256,256]{3,2,1,0:T(8,128)(2,1)} %constant.18.clone.small) | copy-start | bytes 3145732
  28.5 6.8 %collective-permute-start.3 = (bf16[64,1024]{1,0:T(8,128)(2,1)S(1)}, bf16[64,1024]{1,0:T(8,128)(2,1)S(1)}, u32[]{:S(2)}, u32[]{:S(2)}) collective-permute-start(bf16[64,1024]{1,0:T(8,128)(2,1)S(1)} %slices_outer_rows.1), channel_id=1, source_target_pairs={{0,8},{8,16},{16,24},{24,0},{1,9},{9,17},{17,25},{25,1},{2,10},{10... | collective-permute-start | bytes 393224 | tf_op jit(solution)/shard_map/ppermute | solution.py:671
  54.9 21.9 %copy-start.5 = (bf16[2,2,512,512]{3,2,1,0:T(8,128)(2,1)S(1)}, bf16[2,2,512,512]{3,2,1,0:T(8,128)(2,1)}, u32[]{:S(2)}) copy-start(bf16[2,2,512,512]{3,2,1,0:T(8,128)(2,1)} %constant.17.clone.large) | copy-start | bytes 6291460
  54.9 21.9 %copy-start.6 = (bf16[2,4,256,256]{3,2,1,0:T(8,128)(2,1)S(1)}, bf16[2,4,256,256]{3,2,1,0:T(8,128)(2,1)}, u32[]{:S(2)}) copy-start(bf16[2,4,256,256]{3,2,1,0:T(8,128)(2,1)} %constant.16.clone.small) | copy-start | bytes 3145732
